TPU v7x, 512 devices: a whole 4x4x16 slice. The times are simulated.
512 devices in a mesh: row: 32 (over z_lo, y, core), col: 16 (over x, z_hi).
Axes of the slice: x: 4, y: 4, z: 16 (z_hi: 4, z_lo: 4; z = z_hi * 4 + z_lo), core: 2. Of those that a mesh axis runs over, the one named last changes fastest.
Arguments:
- tokens: bfloat16 [384, 6144], P('row', 'col'), may hold values from -6 to 6
- first_weight: bfloat16 [6144, 24576], P('col', 'row'), may hold values from -0.078125 to 0.078125
- first_tangent: bfloat16 [6144, 24576], P('col', 'row'), may hold values from -0.078125 to 0.078125
- second_weight: bfloat16 [24576, 6144], P('row', 'col'), may hold values from -0.0390625 to 0.0390625
- second_tangent: bfloat16 [24576, 6144], P('row', 'col'), may hold values from -0.0390625 to 0.0390625
Outputs:
- first_curvature: bfloat16 [6144, 24576], P('col', 'row')
- second_curvature: bfloat16 [24576, 6144], P('row', 'col')
All inputs are finite; a program needn't handle non-finite values.
Results may differ from a plain program's by a relative error of at most 0.009.
Values may be sent and summed in bfloat16 or wider, within the bound.
No kernel may reach another device: no remote copies, remote signals or barrier semaphores. Data moves between devices by JAX's collectives and lax.ppermute only.
A program may use at most 64 MiB of HBM per device.

v0:
```python
import math

import jax
import jax.numpy as jnp
from jax import lax
from jax.sharding import PartitionSpec as P

sqrt_two_pi = 0.7978845608028654
cubic_coef = 0.044715


def contract_rows(left_side, right_side):
    return lax.dot_general(
        left_side, right_side, (((0,), (0,)), ((), ())), preferred_element_type=jnp.float32
    )


def activate(summed, hidden_width):
    hidden_pre = summed[:, :hidden_width]
    tangent_pre = summed[:, hidden_width:]
    inner_arg = sqrt_two_pi * (hidden_pre + cubic_coef * hidden_pre * hidden_pre * hidden_pre)
    hyper_tan = jnp.tanh(inner_arg)
    activation = (0.5 * hidden_pre * (1.0 + hyper_tan)).astype(jnp.bfloat16)
    derivative = 0.5 * (1.0 + hyper_tan) + 0.5 * hidden_pre * (
        1.0 - hyper_tan * hyper_tan
    ) * sqrt_two_pi * (1.0 + 3.0 * cubic_coef * hidden_pre * hidden_pre)
    tangent_act = (derivative * tangent_pre).astype(jnp.bfloat16)
    return (activation, derivative, tangent_act)


def shards(tokens, first_weight, first_tangent, second_weight, second_tangent):
    gathered = lax.all_gather(tokens, "row", axis=0, tiled=True)
    token_count = gathered.shape[0]
    hidden_width = first_weight.shape[1]
    joined = jnp.concatenate([first_weight, first_tangent], axis=1)
    summed = lax.psum(jnp.dot(gathered, joined, preferred_element_type=jnp.float32), "col")
    activation, derivative, tangent_act = activate(summed, hidden_width)
    tangent_out = lax.psum(
        jnp.dot(tangent_act, second_weight, preferred_element_type=jnp.float32)
        + jnp.dot(activation, second_tangent, preferred_element_type=jnp.float32),
        "row",
    ).astype(jnp.bfloat16)
    grad_act = lax.psum(
        lax.dot_general(
            tangent_out, second_weight, (((1,), (1,)), ((), ())), preferred_element_type=jnp.float32
        ),
        "col",
    )
    grad_pre = (grad_act * derivative).astype(jnp.bfloat16)
    scaling = 1.0 / math.sqrt(token_count)
    first_curvature = (contract_rows(gathered, grad_pre) * scaling).astype(jnp.bfloat16)
    second_curvature = (contract_rows(activation, tangent_out) * scaling).astype(jnp.bfloat16)
    return (first_curvature, second_curvature)


def solution(mesh):
    in_specs = (P("row", "col"), P("col", "row"), P("col", "row"), P("row", "col"), P("row", "col"))
    out_specs = (P("col", "row"), P("row", "col"))
    return jax.shard_map(shards, mesh=mesh, in_specs=in_specs, out_specs=out_specs, check_vma=False)
```

profile of v0, /device:TPU:38, one launch (start us, length us, event | category | flops | bytes accessed | tf_op | source)
XLA Modules:
  0.0 715.3 jit_solution(3307154248823745077)
XLA Ops:
  7.2 0.0 copy-start
  7.2 0.0 copy-start.1
  7.2 0.0 all-reduce.4.cloned.1.call-start
  7.2 38.4 %all-gather = bf16[32,12,384]{2,1,0:T(8,128)(2,1)S(1)} all-gather(bf16[1,12,384]{2,1,0:T(8,128)(2,1)} %bitcast.12), channel_id=1, replica_groups=mesh['row'=32,'col'=16] {'row'}, dimensions={0}, use_global_device_ids=true | all-gather | bytes 304128 | tf_op jit(solution)/shard_map/all_gather | solution.py:32
  45.6 0.1 reshape.5
  45.7 0.0 copy-done.1
  45.7 3.4 convolution_bitcast_fusion
  49.1 0.0 all-reduce.4.cloned.1.call-update
  49.1 0.0 copy-start.4
  49.2 0.0 all-reduce.6.cloned.1.call-start
  49.2 282.2 %all-reduce.4.cloned.1.call-done = f32[384,1536]{0,1:T(8,128)} async-done(((f32[384,1536]{0,1:T(8,128)}), f32[384,1536]{0,1:T(8,128)}) %all-reduce.4.cloned.1.call-update) | async-done | bytes 2359312 | tf_op jit(solution)/shard_map/psum | solution.py:36
  331.4 0.0 copy-done
  331.4 0.0 copy-start.2
  331.4 2.8 fusion.12
  334.3 0.0 copy-done.4
  334.3 0.0 copy-done.2
  334.3 0.6 convolution_add_fusion
  334.9 124.7 %all-reduce.7 = bf16[384,384]{1,0:T(8,128)(2,1)S(1)} all-reduce(f32[384,384]{1,0:T(8,128)S(1)} %convolution_add_fusion), channel_id=1, replica_groups=mesh['row'=32,'col'=16] {'row'}, use_global_device_ids=true, to_apply=%region_1.0 | all-reduce | flops 147456 | bytes 884736 | tf_op jit(solution)/shard_map/psum | solution.py:38
  459.6 0.0 copy-start.3
  459.6 1.6 fusion.20
  461.2 0.0 all-reduce.6.cloned.1.call-update
  461.2 0.5 copy-done.3
  461.7 1.4 fusion.1
  463.1 241.8 %all-reduce.6.cloned.1.call-done = f32[384,768]{0,1:T(8,128)} async-done(((f32[384,768]{0,1:T(8,128)}), f32[384,768]{0,1:T(8,128)}) %all-reduce.6.cloned.1.call-update) | async-done | bytes 1179664 | tf_op jit(solution)/shard_map/psum | solution.py:43
  704.8 2.6 fusion.2
  707.4 1.1 copy.10
Async XLA Ops:
  7.2 324.3 %copy-start = (bf16[768,384]{1,0:T(8,128)(2,1)S(1)}, bf16[768,384]{1,0:T(8,128)(2,1)}, u32[]{:S(2)}) copy-start(bf16[768,384]{1,0:T(8,128)(2,1)} %param.8) | copy-start | bytes 1769476
  7.2 38.5 %copy-start.1 = (bf16[384,768]{1,0:T(8,128)(2,1)S(1)}, bf16[384,768]{1,0:T(8,128)(2,1)}, u32[]{:S(2)}) copy-start(bf16[384,768]{1,0:T(8,128)(2,1)} %param.7) | copy-start | bytes 1769476
  7.2 324.2 %all-reduce.4.cloned.1.call-start = ((), (), s32[]{:S(2)}) async-start(), calls=%async_computation | async-start | bytes 4718592 | tf_op jit(solution)/shard_map/psum | solution.py:36
  49.1 285.1 %copy-start.4 = (bf16[768,384]{1,0:T(8,128)(2,1)S(1)}, bf16[768,384]{1,0:T(8,128)(2,1)}, u32[]{:S(2)}) copy-start(bf16[768,384]{1,0:T(8,128)(2,1)} %param.9) | copy-start | bytes 1769476
  49.2 655.7 %all-reduce.6.cloned.1.call-start = ((), (), s32[]{:S(2)}) async-start(), calls=%async_computation.1 | async-start | bytes 2359296 | tf_op jit(solution)/shard_map/psum | solution.py:43
  331.4 2.9 copy-start.2
  459.6 2.0 copy-start.3
Sparse Core Ops, SparseCore 0:
  49.3 282.1 all-reduce.3
  461.3 243.4 all-reduce.5
where the time goes:
time: 716 us; the launch traced here: 715 us
  waiting for transfers between devices  524 us (73%)
  blocking collectives  163 us (23%)
  between operations  14.1 us (2%)
  matrix products  12.4 us (2%)
    psum x1, waiting for transfers between devices, shards(): lax.psum(jnp.dot(gathered, joined, preferred_element_type=jnp.float32), '...  282 us
    psum x1, waiting for transfers between devices, shards(): lax.psum(lax.dot_general(tangent_out, second_weight, (((1,), (1,)), ((),...  242 us
    psum x1, blocking collectives, shards(): lax.psum(jnp.dot(tangent_act, second_weight, preferred_element_type=jnp.f...  125 us
    all_gather x1, blocking collectives, shards(): gathered = lax.all_gather(tokens, 'row', axis=0, tiled=True)  38.4 us
  transfers between devices with their start and end apart: 2, of which 2 were waited for; matrix products, arithmetic and copies ran while one was open for 0% of the time, Pallas kernels for 0%

commit v1 on v0

v1 whole, which is shorter than its diff:
```python
import math

import jax
import jax.numpy as jnp
from jax import lax
from jax.sharding import Mesh, PartitionSpec as P

sqrt_two_pi = 0.7978845608028654
cubic_coef = 0.044715

ROW = ("z_lo", "y", "core")
f32, bf16 = jnp.float32, jnp.bfloat16


def dot(left_side, right_side, left_dim, right_dim):
    return lax.dot_general(
        left_side, right_side, (((left_dim,), (right_dim,)), ((), ())), preferred_element_type=f32
    )


def swap(blocks, axes):
    return lax.all_to_all(blocks, axes, 0, 0, tiled=True)


def scatter_sum(partial, axes, count):
    arrived = swap(partial.astype(bf16), axes)
    return jnp.sum(arrived.reshape(count, -1, arrived.shape[1]).astype(f32), axis=0)


def gather(block, axes, count):
    return swap(jnp.broadcast_to(block[None], (count,) + block.shape).reshape(-1, block.shape[1]), axes)


def scatter_sum_col(partial):
    return scatter_sum(scatter_sum(partial, "x", 4), "z_hi", 4)


def gather_col(block):
    return gather(gather(block, "z_hi", 4), "x", 4)


def activate(hidden_pre, tangent_pre):
    inner_arg = sqrt_two_pi * (hidden_pre + cubic_coef * hidden_pre * hidden_pre * hidden_pre)
    hyper_tan = jnp.tanh(inner_arg)
    activation = (0.5 * hidden_pre * (1.0 + hyper_tan)).astype(bf16)
    derivative = 0.5 * (1.0 + hyper_tan) + 0.5 * hidden_pre * (
        1.0 - hyper_tan * hyper_tan
    ) * sqrt_two_pi * (1.0 + 3.0 * cubic_coef * hidden_pre * hidden_pre)
    tangent_act = (derivative * tangent_pre).astype(bf16)
    return (activation, derivative, tangent_act)


def shards(tokens, first_weight, first_tangent, second_weight, second_tangent):
    gathered = gather(tokens, ROW, 32)
    token_count = gathered.shape[0]
    width = first_weight.shape[1]
    joined = jnp.concatenate([first_weight, first_tangent], axis=1)
    summed = scatter_sum_col(dot(gathered, joined, 1, 0))
    own_activation, derivative, own_tangent = activate(summed[:, :width], summed[:, width:])
    acts = gather_col(jnp.concatenate([own_activation, own_tangent], axis=1))
    activation, tangent_act = acts[:, :width], acts[:, width:]
    partial_out = dot(tangent_act, second_weight, 1, 0) + dot(activation, second_tangent, 1, 0)
    tangent_out = gather(scatter_sum(partial_out, ROW, 32).astype(bf16), ROW, 32)
    grad_act = scatter_sum_col(dot(tangent_out, second_weight, 1, 1))
    grad_pre = gather_col((grad_act * derivative).astype(bf16))
    scaling = 1.0 / math.sqrt(token_count)
    first_curvature = (dot(gathered, grad_pre, 0, 0) * scaling).astype(bf16)
    second_curvature = (dot(activation, tangent_out, 0, 0) * scaling).astype(bf16)
    return (first_curvature, second_curvature)


def solution(mesh):
    fine = Mesh(mesh.devices.reshape(4, 4, 2, 4, 4), ("z_lo", "y", "core", "x", "z_hi"))
    row, col = ROW, ("x", "z_hi")
    in_specs = (P(row, col), P(col, row), P(col, row), P(row, col), P(row, col))
    out_specs = (P(col, row), P(row, col))
    return jax.shard_map(shards, mesh=fine, in_specs=in_specs, out_specs=out_specs, check_vma=False)
```

time: 716 us -> 223 us (0.31)
  the two profiles are of different devices: /device:TPU:38 before, /device:TPU:32 now
where the time goes in v1:
time: 223 us; the launch traced here: 222 us
  blocking collectives  203 us (91%)
  waiting for transfers between devices  7.01 us (3%)
  matrix products  4.16 us (2%)
  local copies, waits for them, and re-layouts  3.76 us (2%)
  starting transfers between devices  3.48 us (2%)
    all_to_all x10, blocking collectives, swap(): return lax.all_to_all(blocks, axes, 0, 0, tiled=True)  203 us
    all_to_all x1, waiting for transfers between devices, swap(): return lax.all_to_all(blocks, axes, 0, 0, tiled=True)  7.01 us
  transfers between devices with their start and end apart: 1, of which 1 were waited for; matrix products, arithmetic and copies ran while one was open for 1% of the time, Pallas kernels for 0%

profile of v1, /device:TPU:32, one launch (start us, length us, event | category | flops | bytes accessed | tf_op | source)
XLA Modules:
  0.0 222.4 jit_solution(14084384026152823523)
XLA Ops:
  0.6 0.0 copy-start
  0.6 0.0 copy-start.2
  0.7 0.0 copy-start.3
  0.7 0.9 broadcast_in_dim.16
  1.5 21.3 %all_to_all.93 = bf16[32,12,384]{2,1,0:T(8,128)(2,1)S(1)} all-to-all(bf16[32,12,384]{2,1,0:T(8,128)(2,1)S(1)} %broadcast_in_dim.16), channel_id=1, replica_groups=mesh['z_lo'=4,'y'=4,'core'=2,'x'=4,'z_hi'=4] {'z_lo','y','core'}, dimensions={0} | all-to-all | bytes 589824 | tf_op jit(solution)/shard_map/all_to_all | solution.py:22
  22.9 0.1 all_to_all.63
  22.9 0.0 copy-done.2
  22.9 0.0 copy-done.3
  22.9 0.8 convolution_convert_fusion
  23.7 21.1 %all_to_all.94 = bf16[4,96,1536]{2,1,0:T(8,128)(2,1)S(1)} all-to-all(bf16[4,96,1536]{2,1,0:T(8,128)(2,1)S(1)} %bitcast.24), channel_id=1, replica_groups=mesh['z_lo'=4,'y'=4,'core'=2,'x'=4,'z_hi'=4] {'x'}, dimensions={0} | all-to-all | bytes 2359296 | tf_op jit(solution)/shard_map/all_to_all | solution.py:22
  44.9 0.2 reduce_sum.54
  45.0 34.5 %all_to_all.95 = bf16[4,24,1536]{2,1,0:T(8,128)(2,1)S(1)} all-to-all(bf16[4,24,1536]{2,1,0:T(8,128)(2,1)S(1)} %bitcast.25), channel_id=1, replica_groups=mesh['z_lo'=4,'y'=4,'core'=2,'x'=4,'z_hi'=4] {'z_hi'}, dimensions={0} | all-to-all | bytes 589824 | tf_op jit(solution)/shard_map/all_to_all | solution.py:22
  79.6 0.1 multiply_convert_fusion.1
  79.7 23.3 %all_to_all.96 = bf16[4,24,1536]{2,1,0:T(8,128)(2,1)S(1)} all-to-all(bf16[4,24,1536]{2,1,0:T(8,128)(2,1)S(1)} %broadcast_in_dim.17), channel_id=1, replica_groups=mesh['z_lo'=4,'y'=4,'core'=2,'x'=4,'z_hi'=4] {'z_hi'}, dimensions={0} | all-to-all | bytes 589824 | tf_op jit(solution)/shard_map/all_to_all | solution.py:22
  103.0 0.1 broadcast_in_dim.19
  103.1 15.9 %all_to_all.97 = bf16[4,96,1536]{2,1,0:T(8,128)(2,1)S(1)} all-to-all(bf16[4,96,1536]{2,1,0:T(8,128)(2,1)S(1)} %broadcast_in_dim.19), channel_id=1, replica_groups=mesh['z_lo'=4,'y'=4,'core'=2,'x'=4,'z_hi'=4] {'x'}, dimensions={0} | all-to-all | bytes 2359296 | tf_op jit(solution)/shard_map/all_to_all | solution.py:22
  119.1 0.0 copy-start.1
  119.1 0.0 copy-done
  119.1 0.5 fusion.7
  119.5 0.6 copy-done.1
  120.1 0.5 fusion.3
  120.6 0.1 all_to_all.71
  120.7 18.0 %all_to_all.98 = bf16[32,12,384]{2,1,0:T(8,128)(2,1)S(1)} all-to-all(bf16[32,12,384]{2,1,0:T(8,128)(2,1)S(1)} %all_to_all.71), channel_id=1, replica_groups=mesh['z_lo'=4,'y'=4,'core'=2,'x'=4,'z_hi'=4] {'z_lo','y','core'}, dimensions={0} | all-to-all | bytes 589824 | tf_op jit(solution)/shard_map/all_to_all | solution.py:22
  138.6 0.1 reduce_sum.56
  138.8 17.5 %all_to_all.99 = bf16[32,12,384]{2,1,0:T(8,128)(2,1)S(1)} all-to-all(bf16[32,12,384]{2,1,0:T(8,128)(2,1)S(1)} %broadcast_in_dim.20), channel_id=1, replica_groups=mesh['z_lo'=4,'y'=4,'core'=2,'x'=4,'z_hi'=4] {'z_lo','y','core'}, dimensions={0} | all-to-all | bytes 589824 | tf_op jit(solution)/shard_map/all_to_all | solution.py:22
  156.3 0.1 all_to_all.74
  156.4 0.5 convolution_convert_fusion.1
  156.9 13.4 %all_to_all.100 = bf16[4,96,768]{2,1,0:T(8,128)(2,1)S(1)} all-to-all(bf16[4,96,768]{2,1,0:T(8,128)(2,1)S(1)} %bitcast.23), channel_id=1, replica_groups=mesh['z_lo'=4,'y'=4,'core'=2,'x'=4,'z_hi'=4] {'x'}, dimensions={0} | all-to-all | bytes 1179648 | tf_op jit(solution)/shard_map/all_to_all | solution.py:22
  170.2 0.1 reduce_sum.57
  170.3 19.6 %all_to_all.101 = bf16[4,24,768]{2,1,0:T(8,128)(2,1)S(1)} all-to-all(bf16[4,24,768]{2,1,0:T(8,128)(2,1)S(1)} %bitcast.27), channel_id=1, replica_groups=mesh['z_lo'=4,'y'=4,'core'=2,'x'=4,'z_hi'=4] {'z_hi'}, dimensions={0} | all-to-all | bytes 294912 | tf_op jit(solution)/shard_map/all_to_all | solution.py:22
  189.9 0.1 multiply_convert_fusion
  190.0 18.0 %all_to_all.102 = bf16[4,24,768]{2,1,0:T(8,128)(2,1)S(1)} all-to-all(bf16[4,24,768]{2,1,0:T(8,128)(2,1)S(1)} %broadcast_in_dim.21), channel_id=1, replica_groups=mesh['z_lo'=4,'y'=4,'core'=2,'x'=4,'z_hi'=4] {'z_hi'}, dimensions={0} | all-to-all | bytes 294912 | tf_op jit(solution)/shard_map/all_to_all | solution.py:22
  208.0 0.9 broadcast_in_dim.23
  208.9 3.5 %all-to-all-start.10 = ((bf16[4,96,768]{2,1,0:T(8,128)(2,1)}), bf16[4,96,768]{2,1,0:T(8,128)(2,1)S(1)}, u32[]{:S(2)}, u32[]{:S(2)}) async-start(bf16[4,96,768]{2,1,0:T(8,128)(2,1)} %broadcast_in_dim.23), calls=%async_computation.10 | async-start | bytes 1179648 | tf_op jit(solution)/shard_map/all_to_all | solution.py:22
  212.4 1.4 fusion.1
  213.8 7.0 %all-to-all-done.10 = bf16[4,96,768]{2,1,0:T(8,128)(2,1)S(1)} async-done(((bf16[4,96,768]{2,1,0:T(8,128)(2,1)}), bf16[4,96,768]{2,1,0:T(8,128)(2,1)S(1)}, u32[]{:S(2)}, u32[]{:S(2)}) %all-to-all-start.10) | async-done | bytes 589856 | tf_op jit(solution)/shard_map/all_to_all | solution.py:22
  220.8 0.6 fusion.2
  221.4 1.1 copy.9
  (6 shorter events, 0.1 us)
Async XLA Ops:
  0.6 118.4 %copy-start = (bf16[768,384]{1,0:T(8,128)(2,1)S(1)}, bf16[768,384]{1,0:T(8,128)(2,1)}, u32[]{:S(2)}) copy-start(bf16[768,384]{1,0:T(8,128)(2,1)} %param.8) | copy-start | bytes 1769476
  0.6 22.3 %copy-start.2 = (bf16[384,768]{1,0:T(8,128)(2,1)S(1)}, bf16[384,768]{1,0:T(8,128)(2,1)}, u32[]{:S(2)}) copy-start(bf16[384,768]{1,0:T(8,128)(2,1)} %param.7) | copy-start | bytes 1769476
  0.7 22.3 %copy-start.3 = (bf16[384,768]{1,0:T(8,128)(2,1)S(1)}, bf16[384,768]{1,0:T(8,128)(2,1)}, u32[]{:S(2)}) copy-start(bf16[384,768]{1,0:T(8,128)(2,1)} %param.6) | copy-start | bytes 1769476
  119.1 1.1 copy-start.1
  208.9 11.9 %all-to-all-start.10 = ((bf16[4,96,768]{2,1,0:T(8,128)(2,1)}), bf16[4,96,768]{2,1,0:T(8,128)(2,1)S(1)}, u32[]{:S(2)}, u32[]{:S(2)}) async-start(bf16[4,96,768]{2,1,0:T(8,128)(2,1)} %broadcast_in_dim.23), calls=%async_computation.10 | async-start | bytes 1179648 | tf_op jit(solution)/shard_map/all_to_all | solution.py:22

commit v2 on v1

--- a/solution.py
+++ b/solution.py
@@ -31,12 +31,9 @@
     return swap(jnp.broadcast_to(block[None], (count,) + block.shape).reshape(-1, block.shape[1]), axes)
 
 
-def scatter_sum_col(partial):
-    return scatter_sum(scatter_sum(partial, "x", 4), "z_hi", 4)
-
-
-def gather_col(block):
-    return gather(gather(block, "z_hi", 4), "x", 4)
+def exchange_sum(partial, axes, count):
+    arrived = gather(partial.astype(bf16), axes, count)
+    return jnp.sum(arrived.reshape((count,) + partial.shape).astype(f32), axis=0)
 
 
 def activate(hidden_pre, tangent_pre):
@@ -55,14 +52,15 @@
     token_count = gathered.shape[0]
     width = first_weight.shape[1]
     joined = jnp.concatenate([first_weight, first_tangent], axis=1)
-    summed = scatter_sum_col(dot(gathered, joined, 1, 0))
+    summed = exchange_sum(scatter_sum(dot(gathered, joined, 1, 0), "x", 4), "z_hi", 4)
     own_activation, derivative, own_tangent = activate(summed[:, :width], summed[:, width:])
-    acts = gather_col(jnp.concatenate([own_activation, own_tangent], axis=1))
+    acts = gather(jnp.concatenate([own_activation, own_tangent], axis=1), "x", 4)
     activation, tangent_act = acts[:, :width], acts[:, width:]
     partial_out = dot(tangent_act, second_weight, 1, 0) + dot(activation, second_tangent, 1, 0)
-    tangent_out = gather(scatter_sum(partial_out, ROW, 32).astype(bf16), ROW, 32)
-    grad_act = scatter_sum_col(dot(tangent_out, second_weight, 1, 1))
-    grad_pre = gather_col((grad_act * derivative).astype(bf16))
+    out_share = exchange_sum(scatter_sum(partial_out, ("y", "core"), 8), "z_lo", 4).astype(bf16)
+    tangent_out = gather(out_share, ("y", "core"), 8)
+    grad_act = exchange_sum(scatter_sum(dot(tangent_out, second_weight, 1, 1), "x", 4), "z_hi", 4)
+    grad_pre = gather((grad_act * derivative).astype(bf16), "x", 4)
     scaling = 1.0 / math.sqrt(token_count)
     first_curvature = (dot(gathered, grad_pre, 0, 0) * scaling).astype(bf16)
     second_curvature = (dot(activation, tangent_out, 0, 0) * scaling).astype(bf16)

time: 223 us -> 236 us (1.058)
  blocking collectives: 203 us -> 213 us
    all_to_all x10 -> x9, blocking collectives: 203 us -> 213 us  [swap(): return lax.all_to_all(blocks, axes, 0, 0, tiled=True)]
where the time goes in v2:
time: 236 us; the launch traced here: 235 us
  blocking collectives  213 us (90%)
  waiting for transfers between devices  8.72 us (4%)
  matrix products  4.16 us (2%)
  local copies, waits for them, and re-layouts  3.73 us (2%)
  starting transfers between devices  3.48 us (1%)
    all_to_all x9, blocking collectives, swap(): return lax.all_to_all(blocks, axes, 0, 0, tiled=True)  213 us
    all_to_all x1, waiting for transfers between devices, swap(): return lax.all_to_all(blocks, axes, 0, 0, tiled=True)  8.72 us
  transfers between devices with their start and end apart: 1, of which 1 were waited for; matrix products, arithmetic and copies ran while one was open for 1% of the time, Pallas kernels for 0%

profile of v2, /device:TPU:32, one launch (start us, length us, event | category | flops | bytes accessed | tf_op | source)
XLA Modules:
  0.0 235.2 jit_solution(17592643749988755962)
XLA Ops:
  0.6 0.0 copy-start
  0.6 0.0 copy-start.4
  0.7 0.0 copy-start.5
  0.7 0.9 broadcast_in_dim.14
  1.5 21.3 %all_to_all.81 = bf16[32,12,384]{2,1,0:T(8,128)(2,1)S(1)} all-to-all(bf16[32,12,384]{2,1,0:T(8,128)(2,1)S(1)} %broadcast_in_dim.14), channel_id=1, replica_groups=mesh['z_lo'=4,'y'=4,'core'=2,'x'=4,'z_hi'=4] {'z_lo','y','core'}, dimensions={0} | all-to-all | bytes 589824 | tf_op jit(solution)/shard_map/all_to_all | solution.py:22
  22.9 0.1 all_to_all.55
  22.9 0.0 copy-done.4
  22.9 0.0 copy-done.5
  22.9 0.0 copy-start.2
  23.0 0.8 convolution_convert_fusion
  23.7 0.0 copy-done.2
  23.8 21.1 %all_to_all.82 = bf16[4,96,1536]{2,1,0:T(8,128)(2,1)S(1)} all-to-all(bf16[4,96,1536]{2,1,0:T(8,128)(2,1)S(1)} %bitcast.22), channel_id=1, replica_groups=mesh['z_lo'=4,'y'=4,'core'=2,'x'=4,'z_hi'=4] {'x'}, dimensions={0} | all-to-all | bytes 2359296 | tf_op jit(solution)/shard_map/all_to_all | solution.py:22
  44.9 0.2 reduce_sum.66
  45.1 0.1 broadcast_in_dim.15
  45.2 67.1 %all_to_all.83 = bf16[4,96,1536]{2,1,0:T(8,128)(2,1)S(1)} all-to-all(bf16[4,96,1536]{2,1,0:T(8,128)(2,1)S(1)} %broadcast_in_dim.15), channel_id=1, replica_groups=mesh['z_lo'=4,'y'=4,'core'=2,'x'=4,'z_hi'=4] {'z_hi'}, dimensions={0} | all-to-all | bytes 2359296 | tf_op jit(solution)/shard_map/all_to_all | solution.py:22
  112.3 0.2 convert_reduce_fusion
  112.4 0.2 multiply_convert_fusion.1
  112.7 0.1 broadcast_in_dim.16
  112.8 19.4 %all_to_all.84 = bf16[4,96,1536]{2,1,0:T(8,128)(2,1)S(1)} all-to-all(bf16[4,96,1536]{2,1,0:T(8,128)(2,1)S(1)} %broadcast_in_dim.16), channel_id=1, replica_groups=mesh['z_lo'=4,'y'=4,'core'=2,'x'=4,'z_hi'=4] {'x'}, dimensions={0} | all-to-all | bytes 2359296 | tf_op jit(solution)/shard_map/all_to_all | solution.py:22
  132.1 0.0 copy-start.1
  132.1 0.0 copy-done
  132.1 0.5 fusion.7
  132.6 0.6 copy-done.1
  133.2 0.5 fusion.3
  133.7 10.3 %all_to_all.85 = bf16[8,48,384]{2,1,0:T(8,128)(2,1)S(1)} all-to-all(bf16[8,48,384]{2,1,0:T(8,128)(2,1)S(1)} %bitcast.25), channel_id=1, replica_groups=mesh['z_lo'=4,'y'=4,'core'=2,'x'=4,'z_hi'=4] {'y','core'}, dimensions={0} | all-to-all | bytes 589824 | tf_op jit(solution)/shard_map/all_to_all | solution.py:22
  144.0 10.3 %all_to_all.86 = bf16[4,48,384]{2,1,0:T(8,128)(2,1)S(1)} all-to-all(bf16[4,48,384]{2,1,0:T(8,128)(2,1)S(1)} %broadcast_in_dim.17), channel_id=1, replica_groups=mesh['z_lo'=4,'y'=4,'core'=2,'x'=4,'z_hi'=4] {'z_lo'}, dimensions={0} | all-to-all | bytes 294912 | tf_op jit(solution)/shard_map/all_to_all | solution.py:22
  154.4 10.3 %all_to_all.87 = bf16[8,48,384]{2,1,0:T(8,128)(2,1)S(1)} all-to-all(bf16[8,48,384]{2,1,0:T(8,128)(2,1)S(1)} %broadcast_in_dim.18), channel_id=1, replica_groups=mesh['z_lo'=4,'y'=4,'core'=2,'x'=4,'z_hi'=4] {'y','core'}, dimensions={0} | all-to-all | bytes 589824 | tf_op jit(solution)/shard_map/all_to_all | solution.py:22
  164.6 0.5 convolution_convert_fusion.1
  165.1 12.9 %all_to_all.88 = bf16[4,96,768]{2,1,0:T(8,128)(2,1)S(1)} all-to-all(bf16[4,96,768]{2,1,0:T(8,128)(2,1)S(1)} %bitcast.21), channel_id=1, replica_groups=mesh['z_lo'=4,'y'=4,'core'=2,'x'=4,'z_hi'=4] {'x'}, dimensions={0} | all-to-all | bytes 1179648 | tf_op jit(solution)/shard_map/all_to_all | solution.py:22
  178.1 0.1 reduce_sum.70
  178.2 40.6 %all_to_all.89 = bf16[4,96,768]{2,1,0:T(8,128)(2,1)S(1)} all-to-all(bf16[4,96,768]{2,1,0:T(8,128)(2,1)S(1)} %broadcast_in_dim.19), channel_id=1, replica_groups=mesh['z_lo'=4,'y'=4,'core'=2,'x'=4,'z_hi'=4] {'z_hi'}, dimensions={0} | all-to-all | bytes 1179648 | tf_op jit(solution)/shard_map/all_to_all | solution.py:22
  218.8 0.1 convert_reduce_fusion.1
  218.9 0.2 multiply_convert_fusion
  219.1 0.9 broadcast_in_dim.20
  220.0 3.5 %all-to-all-start.9 = ((bf16[4,96,768]{2,1,0:T(8,128)(2,1)}), bf16[4,96,768]{2,1,0:T(8,128)(2,1)S(1)}, u32[]{:S(2)}, u32[]{:S(2)}) async-start(bf16[4,96,768]{2,1,0:T(8,128)(2,1)} %broadcast_in_dim.20), calls=%async_computation.9 | async-start | bytes 1179648 | tf_op jit(solution)/shard_map/all_to_all | solution.py:22
  223.4 0.0 copy-start.3
  223.4 1.4 fusion.1
  224.8 8.7 %all-to-all-done.9 = bf16[4,96,768]{2,1,0:T(8,128)(2,1)S(1)} async-done(((bf16[4,96,768]{2,1,0:T(8,128)(2,1)}), bf16[4,96,768]{2,1,0:T(8,128)(2,1)S(1)}, u32[]{:S(2)}, u32[]{:S(2)}) %all-to-all-start.9) | async-done | bytes 589856 | tf_op jit(solution)/shard_map/all_to_all | solution.py:22
  233.6 0.0 copy-done.3
  233.6 0.6 fusion.2
  234.1 1.1 copy.9
  (6 shorter events, 0.2 us)
Async XLA Ops:
  0.6 131.5 %copy-start = (bf16[768,384]{1,0:T(8,128)(2,1)S(1)}, bf16[768,384]{1,0:T(8,128)(2,1)}, u32[]{:S(2)}) copy-start(bf16[768,384]{1,0:T(8,128)(2,1)} %param.8) | copy-start | bytes 1769476
  0.6 22.3 %copy-start.4 = (bf16[384,768]{1,0:T(8,128)(2,1)S(1)}, bf16[384,768]{1,0:T(8,128)(2,1)}, u32[]{:S(2)}) copy-start(bf16[384,768]{1,0:T(8,128)(2,1)} %param.7) | copy-start | bytes 1769476
  0.7 22.3 %copy-start.5 = (bf16[384,768]{1,0:T(8,128)(2,1)S(1)}, bf16[384,768]{1,0:T(8,128)(2,1)}, u32[]{:S(2)}) copy-start(bf16[384,768]{1,0:T(8,128)(2,1)} %param.6) | copy-start | bytes 1769476
  22.9 0.8 copy-start.2
  132.1 1.1 copy-start.1
  220.0 13.6 %all-to-all-start.9 = ((bf16[4,96,768]{2,1,0:T(8,128)(2,1)}), bf16[4,96,768]{2,1,0:T(8,128)(2,1)S(1)}, u32[]{:S(2)}, u32[]{:S(2)}) async-start(bf16[4,96,768]{2,1,0:T(8,128)(2,1)} %broadcast_in_dim.20), calls=%async_computation.9 | async-start | bytes 1179648 | tf_op jit(solution)/shard_map/all_to_all | solution.py:22
  223.4 10.1 %copy-start.3 = (bf16[384,384]{1,0:T(8,128)(2,1)S(1)}, bf16[384,384]{1,0:T(8,128)(2,1)}, u32[]{:S(2)}) copy-start(bf16[384,384]{1,0:T(8,128)(2,1)} %copy-done.2) | copy-start | bytes 884740

commit v3 on v2

--- a/solution.py
+++ b/solution.py
@@ -47,23 +47,59 @@
     return (activation, derivative, tangent_act)
 
 
+def from_ahead(block, shift):
+    return lax.ppermute(block, "x", [((i + shift) % 4, i) for i in range(4)])
+
+
 def shards(tokens, first_weight, first_tangent, second_weight, second_tangent):
+    together = lax.optimization_barrier
     gathered = gather(tokens, ROW, 32)
+    weight_1, weight_3 = from_ahead(second_weight, 1), from_ahead(second_weight, 3)
+    gathered, weight_1, weight_3 = together((gathered, weight_1, weight_3))
     token_count = gathered.shape[0]
     width = first_weight.shape[1]
     joined = jnp.concatenate([first_weight, first_tangent], axis=1)
-    summed = exchange_sum(scatter_sum(dot(gathered, joined, 1, 0), "x", 4), "z_hi", 4)
+    summed_x = scatter_sum(dot(gathered, joined, 1, 0), "x", 4).astype(bf16)
+    summed_x, second_weight, second_tangent = together((summed_x, second_weight, second_tangent))
+
+    weight_2 = from_ahead(second_weight, 2)
+    tangent_1, tangent_3 = from_ahead(second_tangent, 1), from_ahead(second_tangent, 3)
+    summed = scatter_sum(summed_x, "z_hi", 4)
+    summed, weight_2, tangent_1, tangent_3, second_tangent = together(
+        (summed, weight_2, tangent_1, tangent_3, second_tangent)
+    )
+
+    tangent_2 = from_ahead(second_tangent, 2)
     own_activation, derivative, own_tangent = activate(summed[:, :width], summed[:, width:])
-    acts = gather(jnp.concatenate([own_activation, own_tangent], axis=1), "x", 4)
+    acts = gather(jnp.concatenate([own_activation, own_tangent], axis=1), "z_hi", 4)
+    acts, tangent_2 = together((acts, tangent_2))
+
+    weights = (second_weight, weight_1, weight_2, weight_3)
+    tangents = (second_tangent, tangent_1, tangent_2, tangent_3)
     activation, tangent_act = acts[:, :width], acts[:, width:]
-    partial_out = dot(tangent_act, second_weight, 1, 0) + dot(activation, second_tangent, 1, 0)
-    out_share = exchange_sum(scatter_sum(partial_out, ("y", "core"), 8), "z_lo", 4).astype(bf16)
-    tangent_out = gather(out_share, ("y", "core"), 8)
-    grad_act = exchange_sum(scatter_sum(dot(tangent_out, second_weight, 1, 1), "x", 4), "z_hi", 4)
-    grad_pre = gather((grad_act * derivative).astype(bf16), "x", 4)
+    partial_out = jnp.concatenate(
+        [dot(tangent_act, w, 1, 0) + dot(activation, t, 1, 0) for w, t in zip(weights, tangents)], axis=0
+    ).astype(bf16)
+    partial_out, activation = together((partial_out, activation))
+
+    all_acts = (activation,) + tuple(from_ahead(activation, shift) for shift in (1, 2, 3))
+    share = scatter_sum(partial_out, ("y", "core"), 8)
+    share, all_acts = together((share, all_acts))
+    share = exchange_sum(share, "z_lo", 4).astype(bf16)
+    tangent_out = gather(share, ("y", "core"), 8)
+    outs = jnp.split(tangent_out, 4, axis=0)
+    partial_grad = sum(dot(o, w, 1, 1) for o, w in zip(outs, weights)).astype(bf16)
+    partial_grad, outs = together((partial_grad, outs))
+
+    all_outs = (outs[0],) + tuple(from_ahead(outs[4 - shift], shift) for shift in (1, 2, 3))
+    grad_act = scatter_sum(partial_grad, "z_hi", 4)
+    grad_act, all_outs = together((grad_act, all_outs))
+    grad_pre = gather(gather((grad_act * derivative).astype(bf16), "z_hi", 4), "x", 4)
     scaling = 1.0 / math.sqrt(token_count)
     first_curvature = (dot(gathered, grad_pre, 0, 0) * scaling).astype(bf16)
-    second_curvature = (dot(activation, tangent_out, 0, 0) * scaling).astype(bf16)
+    second_curvature = (
+        dot(jnp.concatenate(all_acts, axis=0), jnp.concatenate(all_outs, axis=0), 0, 0) * scaling
+    ).astype(bf16)
     return (first_curvature, second_curvature)
 
 

time: 236 us -> 248 us (1.051)
  blocking collectives: 213 us -> 65.5 us
  starting transfers between devices: 3.48 us -> 88.4 us
  waiting for transfers between devices: 8.72 us -> 72.4 us
  matrix products: 4.16 us -> 13.7 us
    all_to_all x9 -> x4, blocking collectives: 213 us -> 65.5 us  [swap(): return lax.all_to_all(blocks, axes, 0, 0, tiled=True)]
    all_to_all x1 -> x6, starting transfers between devices: 3.48 us -> 51 us  [swap(): return lax.all_to_all(blocks, axes, 0, 0, tiled=True)]
    ppermute x0 -> x12, waiting for transfers between devices: none -> 41 us  [from_ahead(): return lax.ppermute(block, 'x', [((i + shift) % 4, i) for i in range(4)])]
    ppermute x0 -> x12, starting transfers between devices: none -> 37.4 us  [from_ahead(): return lax.ppermute(block, 'x', [((i + shift) % 4, i) for i in range(4)])]
    all_to_all x1 -> x6, waiting for transfers between devices: 8.72 us -> 31.4 us  [swap(): return lax.all_to_all(blocks, axes, 0, 0, tiled=True)]
    dot_general x6 -> x15, matrix products: 4.16 us -> 13.7 us  [dot(): lax.dot_general(left_side, right_side, (((left_dim,), (right_dim,)), ((),...]
  transfers between devices with their start and end apart: 1 -> 18, of which waited for: 1 -> 12; matrix products, arithmetic and copies ran while one was open for 1% -> 1% of each run, Pallas kernels for 0% -> 0%
where the time goes in v3:
time: 248 us; the launch traced here: 246 us
  starting transfers between devices  88.4 us (36%)
  waiting for transfers between devices  72.4 us (29%)
  blocking collectives  65.5 us (26%)
  matrix products  13.7 us (6%)
  local copies, waits for them, and re-layouts  3.35 us (1%)
    all_to_all x4, blocking collectives, swap(): return lax.all_to_all(blocks, axes, 0, 0, tiled=True)  65.5 us
    all_to_all x6, starting transfers between devices, swap(): return lax.all_to_all(blocks, axes, 0, 0, tiled=True)  51 us
    ppermute x12, waiting for transfers between devices, from_ahead(): return lax.ppermute(block, 'x', [((i + shift) % 4, i) for i in range(4)])  41 us
    ppermute x12, starting transfers between devices, from_ahead(): return lax.ppermute(block, 'x', [((i + shift) % 4, i) for i in range(4)])  37.4 us
    all_to_all x6, waiting for transfers between devices, swap(): return lax.all_to_all(blocks, axes, 0, 0, tiled=True)  31.4 us
    dot_general x15, matrix products, dot(): lax.dot_general(left_side, right_side, (((left_dim,), (right_dim,)), ((),...  13.7 us
  transfers between devices with their start and end apart: 18, of which 12 were waited for; matrix products, arithmetic and copies ran while one was open for 1% of the time, Pallas kernels for 0%

profile of v3, /device:TPU:32, one launch (start us, length us, event | category | flops | bytes accessed | tf_op | source)
XLA Modules:
  0.0 246.3 jit_solution(15177255767255022449)
XLA Ops:
  0.6 1.6 broadcast_in_dim.14
  2.2 9.1 %all-to-all-start = ((bf16[32,12,384]{2,1,0:T(8,128)(2,1)}), bf16[32,12,384]{2,1,0:T(8,128)(2,1)S(1)}, u32[]{:S(2)}, u32[]{:S(2)}) async-start(bf16[32,12,384]{2,1,0:T(8,128)(2,1)} %broadcast_in_dim.14), calls=%async_computation | async-start | bytes 786432 | tf_op jit(solution)/shard_map/all_to_all | solution.py:22
  11.3 4.4 %collective-permute-start = (bf16[768,384]{1,0:T(8,128)(2,1)S(1)}, bf16[768,384]{1,0:T(8,128)(2,1)S(1)}, u32[]{:S(2)}, u32[]{:S(2)}) collective-permute-start(bf16[768,384]{1,0:T(8,128)(2,1)S(1)} %copy-done), channel_id=1, source_target_pairs={{4,0},{8,4},{12,8},{0,12},{5,1},{9,5},{13,9},{1,13},{6,2},{10,6},{... | collective-permute-start | bytes 1769480 | tf_op jit(solution)/shard_map/ppermute | solution.py:51
  15.7 1.9 collective-permute-start.1
  17.6 6.4 %all-to-all-done = bf16[32,12,384]{2,1,0:T(8,128)(2,1)S(1)} async-done(((bf16[32,12,384]{2,1,0:T(8,128)(2,1)}), bf16[32,12,384]{2,1,0:T(8,128)(2,1)S(1)}, u32[]{:S(2)}, u32[]{:S(2)}) %all-to-all-start) | async-done | bytes 294944 | tf_op jit(solution)/shard_map/all_to_all | solution.py:22
  24.2 4.4 %collective-permute-done = bf16[768,384]{1,0:T(8,128)(2,1)S(1)} collective-permute-done((bf16[768,384]{1,0:T(8,128)(2,1)S(1)}, bf16[768,384]{1,0:T(8,128)(2,1)S(1)}, u32[]{:S(2)}, u32[]{:S(2)}) %collective-permute-start) | collective-permute-done | bytes 589856 | tf_op jit(solution)/shard_map/ppermute | solution.py:51
  28.6 5.3 %collective-permute-done.1 = bf16[768,384]{1,0:T(8,128)(2,1)S(1)} collective-permute-done((bf16[768,384]{1,0:T(8,128)(2,1)S(1)}, bf16[768,384]{1,0:T(8,128)(2,1)S(1)}, u32[]{:S(2)}, u32[]{:S(2)}) %collective-permute-start.1) | collective-permute-done | bytes 589856 | tf_op jit(solution)/shard_map/ppermute | solution.py:51
  33.9 1.8 convolution_convert_fusion
  35.8 18.4 %all_to_all.81 = bf16[4,96,1536]{2,1,0:T(8,128)(2,1)S(1)} all-to-all(bf16[4,96,1536]{2,1,0:T(8,128)(2,1)S(1)} %bitcast.39), channel_id=1, replica_groups=mesh['z_lo'=4,'y'=4,'core'=2,'x'=4,'z_hi'=4] {'x'}, dimensions={0} | all-to-all | bytes 2359296 | tf_op jit(solution)/shard_map/all_to_all | solution.py:22
  54.1 0.9 reduce_sum.51
  55.1 12.4 %all-to-all-start.2 = ((bf16[4,24,1536]{2,1,0:T(8,128)(2,1)}), bf16[4,24,1536]{2,1,0:T(8,128)(2,1)S(1)}, u32[]{:S(2)}, u32[]{:S(2)}) async-start(bf16[4,24,1536]{2,1,0:T(8,128)(2,1)} %bitcast.1), calls=%async_computation.2 | async-start | bytes 589824 | tf_op jit(solution)/shard_map/all_to_all | solution.py:22
  67.5 2.7 %collective-permute-start.2 = (bf16[768,384]{1,0:T(8,128)(2,1)S(1)}, bf16[768,384]{1,0:T(8,128)(2,1)S(1)}, u32[]{:S(2)}, u32[]{:S(2)}) collective-permute-start(bf16[768,384]{1,0:T(8,128)(2,1)S(1)} %copy-done), channel_id=1, source_target_pairs={{8,0},{12,4},{0,8},{4,12},{9,1},{13,5},{1,9},{5,13},{10,2},{14,6},... | collective-permute-start | bytes 1769480 | tf_op jit(solution)/shard_map/ppermute | solution.py:51
  70.2 3.1 %collective-permute-start.4 = (bf16[768,384]{1,0:T(8,128)(2,1)}, bf16[768,384]{1,0:T(8,128)(2,1)}, u32[]{:S(2)}, u32[]{:S(2)}) collective-permute-start(bf16[768,384]{1,0:T(8,128)(2,1)} %param.9), channel_id=1, source_target_pairs={{12,0},{0,4},{4,8},{8,12},{13,1},{1,5},{5,9},{9,13},{14,2},{2,6},{... | collective-permute-start | bytes 1769480 | tf_op jit(solution)/shard_map/ppermute | solution.py:51
  73.3 3.9 %collective-permute-start.3 = (bf16[768,384]{1,0:T(8,128)(2,1)}, bf16[768,384]{1,0:T(8,128)(2,1)}, u32[]{:S(2)}, u32[]{:S(2)}) collective-permute-start(bf16[768,384]{1,0:T(8,128)(2,1)} %param.9), channel_id=1, source_target_pairs={{4,0},{8,4},{12,8},{0,12},{5,1},{9,5},{13,9},{1,13},{6,2},{10,6},{... | collective-permute-start | bytes 1769480 | tf_op jit(solution)/shard_map/ppermute | solution.py:51
  77.3 9.5 %all-to-all-done.2 = bf16[4,24,1536]{2,1,0:T(8,128)(2,1)S(1)} async-done(((bf16[4,24,1536]{2,1,0:T(8,128)(2,1)}), bf16[4,24,1536]{2,1,0:T(8,128)(2,1)S(1)}, u32[]{:S(2)}, u32[]{:S(2)}) %all-to-all-start.2) | async-done | bytes 294944 | tf_op jit(solution)/shard_map/all_to_all | solution.py:22
  87.2 9.3 %collective-permute-done.4 = bf16[768,384]{1,0:T(8,128)(2,1)} collective-permute-done((bf16[768,384]{1,0:T(8,128)(2,1)}, bf16[768,384]{1,0:T(8,128)(2,1)}, u32[]{:S(2)}, u32[]{:S(2)}) %collective-permute-start.4) | collective-permute-done | bytes 589856 | tf_op jit(solution)/shard_map/ppermute | solution.py:51
  96.6 0.7 broadcast_in_dim.15
  97.3 11.7 %all-to-all-start.3 = ((bf16[4,24,1536]{2,1,0:T(8,128)(2,1)}), bf16[4,24,1536]{2,1,0:T(8,128)(2,1)S(1)}, u32[]{:S(2)}, u32[]{:S(2)}) async-start(bf16[4,24,1536]{2,1,0:T(8,128)(2,1)} %broadcast_in_dim.15), calls=%async_computation.3 | async-start | bytes 589824 | tf_op jit(solution)/shard_map/all_to_all | solution.py:22
  109.0 3.1 %collective-permute-start.5 = (bf16[768,384]{1,0:T(8,128)(2,1)}, bf16[768,384]{1,0:T(8,128)(2,1)}, u32[]{:S(2)}, u32[]{:S(2)}) collective-permute-start(bf16[768,384]{1,0:T(8,128)(2,1)} %param.9), channel_id=1, source_target_pairs={{8,0},{12,4},{0,8},{4,12},{9,1},{13,5},{1,9},{5,13},{10,2},{14,6},... | collective-permute-start | bytes 1769480 | tf_op jit(solution)/shard_map/ppermute | solution.py:51
  112.2 15.6 %collective-permute-done.5 = bf16[768,384]{1,0:T(8,128)(2,1)} collective-permute-done((bf16[768,384]{1,0:T(8,128)(2,1)}, bf16[768,384]{1,0:T(8,128)(2,1)}, u32[]{:S(2)}, u32[]{:S(2)}) %collective-permute-start.5) | collective-permute-done | bytes 589856 | tf_op jit(solution)/shard_map/ppermute | solution.py:51
  127.7 3.5 %all-to-all-done.3 = bf16[4,24,1536]{2,1,0:T(8,128)(2,1)S(1)} async-done(((bf16[4,24,1536]{2,1,0:T(8,128)(2,1)}), bf16[4,24,1536]{2,1,0:T(8,128)(2,1)S(1)}, u32[]{:S(2)}, u32[]{:S(2)}) %all-to-all-start.3) | async-done | bytes 294944 | tf_op jit(solution)/shard_map/all_to_all | solution.py:22
  131.2 1.3 fusion.42
  132.6 1.4 fusion.40
  134.0 1.3 fusion.36
  135.3 1.3 fusion.38
  137.7 0.7 pad_maximum_fusion
  138.4 4.2 %all-to-all-start.4 = ((bf16[8,48,384]{2,1,0:T(8,128)(2,1)}), bf16[8,48,384]{2,1,0:T(8,128)(2,1)S(1)}, u32[]{:S(2)}, u32[]{:S(2)}) async-start(bf16[8,48,384]{2,1,0:T(8,128)(2,1)} %bitcast.3), calls=%async_computation.4 | async-start | bytes 589824 | tf_op jit(solution)/shard_map/all_to_all | solution.py:22
  142.6 2.5 collective-permute-start.8
  145.1 3.3 %collective-permute-start.7 = (bf16[96,768]{1,0:T(8,128)(2,1)S(1)}, bf16[96,768]{1,0:T(8,128)(2,1)S(1)}, u32[]{:S(2)}, u32[]{:S(2)}) collective-permute-start(bf16[96,768]{1,0:T(8,128)(2,1)S(1)} %slice.19), channel_id=1, source_target_pairs={{8,0},{12,4},{0,8},{4,12},{9,1},{13,5},{1,9},{5,13},{10,2},{14,6},... | collective-permute-start | bytes 442376 | tf_op jit(solution)/shard_map/ppermute | solution.py:51
  148.4 3.2 %collective-permute-start.6 = (bf16[96,768]{1,0:T(8,128)(2,1)S(1)}, bf16[96,768]{1,0:T(8,128)(2,1)}, u32[]{:S(2)}, u32[]{:S(2)}) collective-permute-start(bf16[96,768]{1,0:T(8,128)(2,1)S(1)} %slice.19), channel_id=1, source_target_pairs={{4,0},{8,4},{12,8},{0,12},{5,1},{9,5},{13,9},{1,13},{6,2},{10,6},{... | collective-permute-start | bytes 442376 | tf_op jit(solution)/shard_map/ppermute | solution.py:51
  151.6 3.5 %collective-permute-done.8 = bf16[96,768]{1,0:T(8,128)(2,1)S(1)} collective-permute-done((bf16[96,768]{1,0:T(8,128)(2,1)S(1)}, bf16[96,768]{1,0:T(8,128)(2,1)S(1)}, u32[]{:S(2)}, u32[]{:S(2)}) %collective-permute-start.8) | collective-permute-done | bytes 147488 | tf_op jit(solution)/shard_map/ppermute | solution.py:51
  155.1 2.6 %collective-permute-done.6 = bf16[96,768]{1,0:T(8,128)(2,1)} collective-permute-done((bf16[96,768]{1,0:T(8,128)(2,1)S(1)}, bf16[96,768]{1,0:T(8,128)(2,1)}, u32[]{:S(2)}, u32[]{:S(2)}) %collective-permute-start.6) | collective-permute-done | bytes 147488 | tf_op jit(solution)/shard_map/ppermute | solution.py:51
  157.7 8.4 %all_to_all.82 = bf16[4,48,384]{2,1,0:T(8,128)(2,1)S(1)} all-to-all(bf16[4,48,384]{2,1,0:T(8,128)(2,1)S(1)} %broadcast_in_dim.16), channel_id=1, replica_groups=mesh['z_lo'=4,'y'=4,'core'=2,'x'=4,'z_hi'=4] {'z_lo'}, dimensions={0} | all-to-all | bytes 294912 | tf_op jit(solution)/shard_map/all_to_all | solution.py:22
  166.2 12.1 %all_to_all.83 = bf16[8,48,384]{2,1,0:T(8,128)(2,1)S(1)} all-to-all(bf16[8,48,384]{2,1,0:T(8,128)(2,1)S(1)} %broadcast_in_dim.17), channel_id=1, replica_groups=mesh['z_lo'=4,'y'=4,'core'=2,'x'=4,'z_hi'=4] {'y','core'}, dimensions={0} | all-to-all | bytes 589824 | tf_op jit(solution)/shard_map/all_to_all | solution.py:22
  178.3 0.3 fusion.46
  179.0 0.3 convolution_add_fusion.1
  179.3 1.0 fusion.6
  180.3 10.2 %all-to-all-start.7 = ((bf16[4,24,768]{2,1,0:T(8,128)(2,1)}), bf16[4,24,768]{2,1,0:T(8,128)(2,1)S(1)}, u32[]{:S(2)}, u32[]{:S(2)}) async-start(bf16[4,24,768]{2,1,0:T(8,128)(2,1)} %bitcast.8), calls=%async_computation.7 | async-start | bytes 294912 | tf_op jit(solution)/shard_map/all_to_all | solution.py:22
  190.4 4.6 %collective-permute-start.9 = (bf16[96,384]{1,0:T(8,128)(2,1)S(1)}, bf16[96,384]{1,0:T(8,128)(2,1)S(1)}, u32[]{:S(2)}, u32[]{:S(2)}) collective-permute-start(bf16[96,384]{1,0:T(8,128)(2,1)S(1)} %bitcast.49), channel_id=1, source_target_pairs={{4,0},{8,4},{12,8},{0,12},{5,1},{9,5},{13,9},{1,13},{6,2},{10,6},{... | collective-permute-start | bytes 221192 | tf_op jit(solution)/shard_map/ppermute | solution.py:51
  195.0 1.9 collective-permute-start.10
  196.9 2.8 %collective-permute-start.11 = (bf16[96,384]{1,0:T(8,128)(2,1)S(1)}, bf16[96,384]{1,0:T(8,128)(2,1)S(1)}, u32[]{:S(2)}, u32[]{:S(2)}) collective-permute-start(bf16[96,384]{1,0:T(8,128)(2,1)S(1)} %bitcast.43), channel_id=1, source_target_pairs={{12,0},{0,4},{4,8},{8,12},{13,1},{1,5},{5,9},{9,13},{14,2},{2,6},{... | collective-permute-start | bytes 221192 | tf_op jit(solution)/shard_map/ppermute | solution.py:51
  199.7 5.8 %all-to-all-done.7 = bf16[4,24,768]{2,1,0:T(8,128)(2,1)S(1)} async-done(((bf16[4,24,768]{2,1,0:T(8,128)(2,1)}), bf16[4,24,768]{2,1,0:T(8,128)(2,1)S(1)}, u32[]{:S(2)}, u32[]{:S(2)}) %all-to-all-start.7) | async-done | bytes 147488 | tf_op jit(solution)/shard_map/all_to_all | solution.py:22
  205.7 26.6 %all_to_all.84 = bf16[4,24,768]{2,1,0:T(8,128)(2,1)S(1)} all-to-all(bf16[4,24,768]{2,1,0:T(8,128)(2,1)S(1)} %broadcast_in_dim.18), channel_id=1, replica_groups=mesh['z_lo'=4,'y'=4,'core'=2,'x'=4,'z_hi'=4] {'z_hi'}, dimensions={0} | all-to-all | bytes 294912 | tf_op jit(solution)/shard_map/all_to_all | solution.py:22
  232.3 0.9 broadcast_in_dim.20
  233.1 3.5 %all-to-all-start.9 = ((bf16[4,96,768]{2,1,0:T(8,128)(2,1)}), bf16[4,96,768]{2,1,0:T(8,128)(2,1)S(1)}, u32[]{:S(2)}, u32[]{:S(2)}) async-start(bf16[4,96,768]{2,1,0:T(8,128)(2,1)} %broadcast_in_dim.20), calls=%async_computation.9 | async-start | bytes 1179648 | tf_op jit(solution)/shard_map/all_to_all | solution.py:22
  236.6 2.3 fusion.1
  238.9 6.1 %all-to-all-done.9 = bf16[4,96,768]{2,1,0:T(8,128)(2,1)S(1)} async-done(((bf16[4,96,768]{2,1,0:T(8,128)(2,1)}), bf16[4,96,768]{2,1,0:T(8,128)(2,1)S(1)}, u32[]{:S(2)}, u32[]{:S(2)}) %all-to-all-start.9) | async-done | bytes 589856 | tf_op jit(solution)/shard_map/all_to_all | solution.py:22
  245.0 1.3 fusion
  (33 shorter events, 2.1 us)
Async XLA Ops:
  0.6 10.7 %copy-start = (bf16[768,384]{1,0:T(8,128)(2,1)S(1)}, bf16[768,384]{1,0:T(8,128)(2,1)}, u32[]{:S(2)}) copy-start(bf16[768,384]{1,0:T(8,128)(2,1)} %param.8) | copy-start | bytes 1769476
  0.6 33.3 %copy-start.3 = (bf16[384,768]{1,0:T(8,128)(2,1)S(1)}, bf16[384,768]{1,0:T(8,128)(2,1)}, u32[]{:S(2)}) copy-start(bf16[384,768]{1,0:T(8,128)(2,1)} %param.7) | copy-start | bytes 1769476
  2.2 21.9 %all-to-all-start = ((bf16[32,12,384]{2,1,0:T(8,128)(2,1)}), bf16[32,12,384]{2,1,0:T(8,128)(2,1)S(1)}, u32[]{:S(2)}, u32[]{:S(2)}) async-start(bf16[32,12,384]{2,1,0:T(8,128)(2,1)} %broadcast_in_dim.14), calls=%async_computation | async-start | bytes 786432 | tf_op jit(solution)/shard_map/all_to_all | solution.py:22
  11.3 17.3 %collective-permute-start = (bf16[768,384]{1,0:T(8,128)(2,1)S(1)}, bf16[768,384]{1,0:T(8,128)(2,1)S(1)}, u32[]{:S(2)}, u32[]{:S(2)}) collective-permute-start(bf16[768,384]{1,0:T(8,128)(2,1)S(1)} %copy-done), channel_id=1, source_target_pairs={{4,0},{8,4},{12,8},{0,12},{5,1},{9,5},{13,9},{1,13},{6,2},{10,6},{... | collective-permute-start | bytes 1769480 | tf_op jit(solution)/shard_map/ppermute | solution.py:51
  15.7 18.2 %collective-permute-start.1 = (bf16[768,384]{1,0:T(8,128)(2,1)S(1)}, bf16[768,384]{1,0:T(8,128)(2,1)S(1)}, u32[]{:S(2)}, u32[]{:S(2)}) collective-permute-start(bf16[768,384]{1,0:T(8,128)(2,1)S(1)} %copy-done), channel_id=1, source_target_pairs={{12,0},{0,4},{4,8},{8,12},{13,1},{1,5},{5,9},{9,13},{14,2},{2,6},{... | collective-permute-start | bytes 1769480 | tf_op jit(solution)/shard_map/ppermute | solution.py:51
  55.1 31.7 %all-to-all-start.2 = ((bf16[4,24,1536]{2,1,0:T(8,128)(2,1)}), bf16[4,24,1536]{2,1,0:T(8,128)(2,1)S(1)}, u32[]{:S(2)}, u32[]{:S(2)}) async-start(bf16[4,24,1536]{2,1,0:T(8,128)(2,1)} %bitcast.1), calls=%async_computation.2 | async-start | bytes 589824 | tf_op jit(solution)/shard_map/all_to_all | solution.py:22
  67.5 19.7 %collective-permute-start.2 = (bf16[768,384]{1,0:T(8,128)(2,1)S(1)}, bf16[768,384]{1,0:T(8,128)(2,1)S(1)}, u32[]{:S(2)}, u32[]{:S(2)}) collective-permute-start(bf16[768,384]{1,0:T(8,128)(2,1)S(1)} %copy-done), channel_id=1, source_target_pairs={{8,0},{12,4},{0,8},{4,12},{9,1},{13,5},{1,9},{5,13},{10,2},{14,6},... | collective-permute-start | bytes 1769480 | tf_op jit(solution)/shard_map/ppermute | solution.py:51
  70.2 26.3 %collective-permute-start.4 = (bf16[768,384]{1,0:T(8,128)(2,1)}, bf16[768,384]{1,0:T(8,128)(2,1)}, u32[]{:S(2)}, u32[]{:S(2)}) collective-permute-start(bf16[768,384]{1,0:T(8,128)(2,1)} %param.9), channel_id=1, source_target_pairs={{12,0},{0,4},{4,8},{8,12},{13,1},{1,5},{5,9},{9,13},{14,2},{2,6},{... | collective-permute-start | bytes 1769480 | tf_op jit(solution)/shard_map/ppermute | solution.py:51
  73.3 23.2 %collective-permute-start.3 = (bf16[768,384]{1,0:T(8,128)(2,1)}, bf16[768,384]{1,0:T(8,128)(2,1)}, u32[]{:S(2)}, u32[]{:S(2)}) collective-permute-start(bf16[768,384]{1,0:T(8,128)(2,1)} %param.9), channel_id=1, source_target_pairs={{4,0},{8,4},{12,8},{0,12},{5,1},{9,5},{13,9},{1,13},{6,2},{10,6},{... | collective-permute-start | bytes 1769480 | tf_op jit(solution)/shard_map/ppermute | solution.py:51
  97.3 33.9 %all-to-all-start.3 = ((bf16[4,24,1536]{2,1,0:T(8,128)(2,1)}), bf16[4,24,1536]{2,1,0:T(8,128)(2,1)S(1)}, u32[]{:S(2)}, u32[]{:S(2)}) async-start(bf16[4,24,1536]{2,1,0:T(8,128)(2,1)} %broadcast_in_dim.15), calls=%async_computation.3 | async-start | bytes 589824 | tf_op jit(solution)/shard_map/all_to_all | solution.py:22
  109.0 18.7 %collective-permute-start.5 = (bf16[768,384]{1,0:T(8,128)(2,1)}, bf16[768,384]{1,0:T(8,128)(2,1)}, u32[]{:S(2)}, u32[]{:S(2)}) collective-permute-start(bf16[768,384]{1,0:T(8,128)(2,1)} %param.9), channel_id=1, source_target_pairs={{8,0},{12,4},{0,8},{4,12},{9,1},{13,5},{1,9},{5,13},{10,2},{14,6},... | collective-permute-start | bytes 1769480 | tf_op jit(solution)/shard_map/ppermute | solution.py:51
  132.6 15.8 %copy-start.1 = (bf16[96,768]{1,0:T(8,128)(2,1)}, bf16[96,768]{1,0:T(8,128)(2,1)S(1)}, u32[]{:S(2)}) copy-start(bf16[96,768]{1,0:T(8,128)(2,1)S(1)} %slice.19) | copy-start | bytes 442372
  138.4 13.2 %all-to-all-start.4 = ((bf16[8,48,384]{2,1,0:T(8,128)(2,1)}), bf16[8,48,384]{2,1,0:T(8,128)(2,1)S(1)}, u32[]{:S(2)}, u32[]{:S(2)}) async-start(bf16[8,48,384]{2,1,0:T(8,128)(2,1)} %bitcast.3), calls=%async_computation.4 | async-start | bytes 589824 | tf_op jit(solution)/shard_map/all_to_all | solution.py:22
  142.6 12.5 %collective-permute-start.8 = (bf16[96,768]{1,0:T(8,128)(2,1)S(1)}, bf16[96,768]{1,0:T(8,128)(2,1)S(1)}, u32[]{:S(2)}, u32[]{:S(2)}) collective-permute-start(bf16[96,768]{1,0:T(8,128)(2,1)S(1)} %slice.19), channel_id=1, source_target_pairs={{12,0},{0,4},{4,8},{8,12},{13,1},{1,5},{5,9},{9,13},{14,2},{2,6},{... | collective-permute-start | bytes 442376 | tf_op jit(solution)/shard_map/ppermute | solution.py:51
  145.1 10.0 %collective-permute-start.7 = (bf16[96,768]{1,0:T(8,128)(2,1)S(1)}, bf16[96,768]{1,0:T(8,128)(2,1)S(1)}, u32[]{:S(2)}, u32[]{:S(2)}) collective-permute-start(bf16[96,768]{1,0:T(8,128)(2,1)S(1)} %slice.19), channel_id=1, source_target_pairs={{8,0},{12,4},{0,8},{4,12},{9,1},{13,5},{1,9},{5,13},{10,2},{14,6},... | collective-permute-start | bytes 442376 | tf_op jit(solution)/shard_map/ppermute | solution.py:51
  148.4 9.3 %collective-permute-start.6 = (bf16[96,768]{1,0:T(8,128)(2,1)S(1)}, bf16[96,768]{1,0:T(8,128)(2,1)}, u32[]{:S(2)}, u32[]{:S(2)}) collective-permute-start(bf16[96,768]{1,0:T(8,128)(2,1)S(1)} %slice.19), channel_id=1, source_target_pairs={{4,0},{8,4},{12,8},{0,12},{5,1},{9,5},{13,9},{1,13},{6,2},{10,6},{... | collective-permute-start | bytes 442376 | tf_op jit(solution)/shard_map/ppermute | solution.py:51
  180.3 25.3 %all-to-all-start.7 = ((bf16[4,24,768]{2,1,0:T(8,128)(2,1)}), bf16[4,24,768]{2,1,0:T(8,128)(2,1)S(1)}, u32[]{:S(2)}, u32[]{:S(2)}) async-start(bf16[4,24,768]{2,1,0:T(8,128)(2,1)} %bitcast.8), calls=%async_computation.7 | async-start | bytes 294912 | tf_op jit(solution)/shard_map/all_to_all | solution.py:22
  190.4 15.1 %collective-permute-start.9 = (bf16[96,384]{1,0:T(8,128)(2,1)S(1)}, bf16[96,384]{1,0:T(8,128)(2,1)S(1)}, u32[]{:S(2)}, u32[]{:S(2)}) collective-permute-start(bf16[96,384]{1,0:T(8,128)(2,1)S(1)} %bitcast.49), channel_id=1, source_target_pairs={{4,0},{8,4},{12,8},{0,12},{5,1},{9,5},{13,9},{1,13},{6,2},{10,6},{... | collective-permute-start | bytes 221192 | tf_op jit(solution)/shard_map/ppermute | solution.py:51
  195.0 10.6 %collective-permute-start.10 = (bf16[96,384]{1,0:T(8,128)(2,1)S(1)}, bf16[96,384]{1,0:T(8,128)(2,1)S(1)}, u32[]{:S(2)}, u32[]{:S(2)}) collective-permute-start(bf16[96,384]{1,0:T(8,128)(2,1)S(1)} %bitcast.45), channel_id=1, source_target_pairs={{8,0},{12,4},{0,8},{4,12},{9,1},{13,5},{1,9},{5,13},{10,2},{14,6},... | collective-permute-start | bytes 221192 | tf_op jit(solution)/shard_map/ppermute | solution.py:51
  196.9 8.6 %collective-permute-start.11 = (bf16[96,384]{1,0:T(8,128)(2,1)S(1)}, bf16[96,384]{1,0:T(8,128)(2,1)S(1)}, u32[]{:S(2)}, u32[]{:S(2)}) collective-permute-start(bf16[96,384]{1,0:T(8,128)(2,1)S(1)} %bitcast.43), channel_id=1, source_target_pairs={{12,0},{0,4},{4,8},{8,12},{13,1},{1,5},{5,9},{9,13},{14,2},{2,6},{... | collective-permute-start | bytes 221192 | tf_op jit(solution)/shard_map/ppermute | solution.py:51
  205.7 30.9 %copy-start.2 = (bf16[96,768]{1,0:T(8,128)(2,1)S(1)}, bf16[96,768]{1,0:T(8,128)(2,1)}, u32[]{:S(2)}) copy-start(bf16[96,768]{1,0:T(8,128)(2,1)} %copy-done.1) | copy-start | bytes 442372
  233.1 11.9 %all-to-all-start.9 = ((bf16[4,96,768]{2,1,0:T(8,128)(2,1)}), bf16[4,96,768]{2,1,0:T(8,128)(2,1)S(1)}, u32[]{:S(2)}, u32[]{:S(2)}) async-start(bf16[4,96,768]{2,1,0:T(8,128)(2,1)} %broadcast_in_dim.20), calls=%async_computation.9 | async-start | bytes 1179648 | tf_op jit(solution)/shard_map/all_to_all | solution.py:22

commit v4 on v2

--- a/solution.py
+++ b/solution.py
@@ -3,6 +3,8 @@
 import jax
 import jax.numpy as jnp
 from jax import lax
+from jax.experimental import pallas as pl
+from jax.experimental.pallas import tpu as pltpu
 from jax.sharding import Mesh, PartitionSpec as P
 
 sqrt_two_pi = 0.7978845608028654
@@ -47,23 +49,77 @@
     return (activation, derivative, tangent_act)
 
 
+def mm(left_side, right_side, left_dim, right_dim):
+    return lax.dot_general(
+        left_side, right_side, (((left_dim,), (right_dim,)), ((), ())), preferred_element_type=f32
+    )
+
+
+def out_kernel(acts_ref, tangents_ref, rest_ref, out_ref, copy_ref):
+    head = tangents_ref.shape[1]
+    width = acts_ref.shape[1] // 2
+    activation, tangent_act = acts_ref[:, :width], acts_ref[:, width:]
+    copy_ref[...] = acts_ref[...]
+    for block in range(4):
+        total = mm(tangent_act, rest_ref[block, :width], 1, 0)
+        total += mm(activation[:, :head], tangents_ref[block], 1, 0)
+        total += mm(activation[:, head:], rest_ref[block, width:], 1, 0)
+        out_ref[block] = total.astype(bf16)
+
+
+def grad_kernel(out_ref, rest_ref, grad_ref):
+    width = grad_ref.shape[1]
+    total = mm(out_ref[0], rest_ref[0, :width], 1, 1)
+    for block in range(1, 4):
+        total += mm(out_ref[block], rest_ref[block, :width], 1, 1)
+    grad_ref[...] = total.astype(bf16)
+
+
+PARAMS = pltpu.CompilerParams(vmem_limit_bytes=32 * 1024 * 1024)
+
+
 def shards(tokens, first_weight, first_tangent, second_weight, second_tangent):
+    together = lax.optimization_barrier
+    width, features = second_weight.shape
+    head = width // 4 * 3
+    tangents = lax.all_gather(second_tangent[:head], "x")
     gathered = gather(tokens, ROW, 32)
     token_count = gathered.shape[0]
-    width = first_weight.shape[1]
     joined = jnp.concatenate([first_weight, first_tangent], axis=1)
-    summed = exchange_sum(scatter_sum(dot(gathered, joined, 1, 0), "x", 4), "z_hi", 4)
+    summed_x = scatter_sum(dot(gathered, joined, 1, 0), "x", 4).astype(bf16)
+    rest = jnp.concatenate([second_weight, second_tangent[head:]], axis=0)
+    summed_x, rest = together((summed_x, rest))
+
+    rest = lax.all_gather(rest, "x")
+    summed = scatter_sum(summed_x, "z_hi", 4)
     own_activation, derivative, own_tangent = activate(summed[:, :width], summed[:, width:])
-    acts = gather(jnp.concatenate([own_activation, own_tangent], axis=1), "x", 4)
-    activation, tangent_act = acts[:, :width], acts[:, width:]
-    partial_out = dot(tangent_act, second_weight, 1, 0) + dot(activation, second_tangent, 1, 0)
-    out_share = exchange_sum(scatter_sum(partial_out, ("y", "core"), 8), "z_lo", 4).astype(bf16)
-    tangent_out = gather(out_share, ("y", "core"), 8)
-    grad_act = exchange_sum(scatter_sum(dot(tangent_out, second_weight, 1, 1), "x", 4), "z_hi", 4)
-    grad_pre = gather((grad_act * derivative).astype(bf16), "x", 4)
+    acts = gather(jnp.concatenate([own_activation, own_tangent], axis=1), "z_hi", 4)
+
+    share_rows = acts.shape[0]
+    partial_out, acts = pl.pallas_call(
+        out_kernel,
+        out_shape=(
+            jax.ShapeDtypeStruct((4, share_rows, features), bf16),
+            jax.ShapeDtypeStruct(acts.shape, bf16),
+        ),
+        compiler_params=PARAMS,
+    )(acts, tangents, rest)
+    all_acts = lax.all_gather(acts, "x", tiled=True)
+    share = scatter_sum(partial_out.reshape(-1, features), ("y", "core"), 8)
+    share = exchange_sum(share, "z_lo", 4).astype(bf16)
+    tangent_out = gather(share, ("y", "core"), 8)
+    tangent_out, all_acts = together((tangent_out, all_acts))
+    outs = tangent_out.reshape(4, share_rows, features)
+    partial_grad = pl.pallas_call(
+        grad_kernel, out_shape=jax.ShapeDtypeStruct((share_rows, width), bf16), compiler_params=PARAMS
+    )(outs, rest)
+    grad_act = scatter_sum(partial_grad, "z_hi", 4)
+    grad_pre = gather((grad_act * derivative).astype(bf16), "z_hi", 4)
+    grad_copies = jnp.broadcast_to(grad_pre[None], (4,) + grad_pre.shape)
+    final = swap(jnp.concatenate([grad_copies, outs], axis=2), "x").reshape(token_count, -1)
     scaling = 1.0 / math.sqrt(token_count)
-    first_curvature = (dot(gathered, grad_pre, 0, 0) * scaling).astype(bf16)
-    second_curvature = (dot(activation, tangent_out, 0, 0) * scaling).astype(bf16)
+    first_curvature = (dot(gathered, final[:, :width], 0, 0) * scaling).astype(bf16)
+    second_curvature = (dot(all_acts[:, :width], final[:, width:], 0, 0) * scaling).astype(bf16)
     return (first_curvature, second_curvature)
 
 

time: 236 us -> 222 us (0.941)
  the two profiles are of different devices: /device:TPU:32 before, /device:TPU:8 now
where the time goes in v4:
time: 222 us; the launch traced here: 221 us
  blocking collectives  140 us (63%)
  waiting for transfers between devices  42.5 us (19%)
  between operations  13.9 us (6%)
  starting transfers between devices  9.15 us (4%)
  local copies, waits for them, and re-layouts  8.54 us (4%)
  matrix products  3.77 us (2%)
  Pallas kernels  2.43 us (1%)
    all_to_all x8, blocking collectives, swap(): return lax.all_to_all(blocks, axes, 0, 0, tiled=True)  140 us
    all_to_all x2, waiting for transfers between devices, swap(): return lax.all_to_all(blocks, axes, 0, 0, tiled=True)  42.5 us
    all_to_all x2, starting transfers between devices, swap(): return lax.all_to_all(blocks, axes, 0, 0, tiled=True)  9.11 us
    unnamed x25, local copies, waits for them, and re-layouts  5.77 us
  transfers between devices with their start and end apart: 5, of which 2 were waited for; matrix products, arithmetic and copies ran while one was open for 2% of the time, Pallas kernels for 0%

profile of v4, /device:TPU:8, one launch (start us, length us, event | category | flops | bytes accessed | tf_op | source)
XLA Modules:
  0.0 221.3 jit_solution(5067183345734445432)
XLA Ops:
  7.2 0.0 copy-start.8
  7.2 0.0 all-gather.8.cloned.1.call-start
  7.2 1.8 slice.24
  9.0 0.0 all-gather.8.cloned.1.call-update
  9.1 0.0 copy-done.8
  9.1 21.0 %all_to_all.79 = bf16[32,12,384]{2,1,0:T(8,128)(2,1)S(1)} all-to-all(bf16[32,12,384]{2,1,0:T(8,128)(2,1)S(1)} %broadcast_in_dim.14), channel_id=1, replica_groups=mesh['z_lo'=4,'y'=4,'core'=2,'x'=4,'z_hi'=4] {'z_lo','y','core'}, dimensions={0} | all-to-all | bytes 589824 | tf_op jit(solution)/shard_map/all_to_all | solution.py:24
  30.1 0.1 all_to_all.53
  30.2 0.0 copy-done.10
  30.2 0.0 copy-done.11
  30.2 0.0 copy-start.6
  30.2 1.8 convolution_convert_fusion
  32.0 0.0 copy-done.6
  32.0 4.4 %all-to-all-start.1 = ((bf16[4,96,1536]{2,1,0:T(8,128)(2,1)}), bf16[4,96,1536]{2,1,0:T(8,128)(2,1)S(1)}, u32[]{:S(2)}, u32[]{:S(2)}) async-start(bf16[4,96,1536]{2,1,0:T(8,128)(2,1)} %bitcast.1), calls=%async_computation.1 | async-start | bytes 2359296 | tf_op jit(solution)/shard_map/all_to_all | solution.py:24
  36.4 0.0 all-gather.10.cloned.1.call-start
  36.4 0.0 slice-done
  36.4 0.0 copy-done.5
  36.4 1.0 pad_maximum_fusion.1
  37.4 26.0 %all-to-all-done.1 = bf16[4,96,1536]{2,1,0:T(8,128)(2,1)S(1)} async-done(((bf16[4,96,1536]{2,1,0:T(8,128)(2,1)}), bf16[4,96,1536]{2,1,0:T(8,128)(2,1)S(1)}, u32[]{:S(2)}, u32[]{:S(2)}) %all-to-all-start.1) | async-done | bytes 1179680 | tf_op jit(solution)/shard_map/all_to_all | solution.py:24
  63.4 0.2 reduce_sum.54
  63.6 0.0 all-gather.10.cloned.1.call-update
  63.6 32.7 %all_to_all.80 = bf16[4,24,1536]{2,1,0:T(8,128)(2,1)S(1)} all-to-all(bf16[4,24,1536]{2,1,0:T(8,128)(2,1)S(1)} %bitcast.25), channel_id=1, replica_groups=mesh['z_lo'=4,'y'=4,'core'=2,'x'=4,'z_hi'=4] {'z_hi'}, dimensions={0} | all-to-all | bytes 589824 | tf_op jit(solution)/shard_map/all_to_all | solution.py:24
  96.4 0.0 copy-start.3
  96.4 0.7 copy-done.3
  97.1 0.1 multiply_convert_fusion.1
  97.1 0.7 broadcast_in_dim.15
  97.9 4.7 %all-to-all-start.3 = ((bf16[4,24,1536]{2,1,0:T(8,128)(2,1)}), bf16[4,24,1536]{2,1,0:T(8,128)(2,1)S(1)}, u32[]{:S(2)}, u32[]{:S(2)}) async-start(bf16[4,24,1536]{2,1,0:T(8,128)(2,1)} %broadcast_in_dim.15), calls=%async_computation.3 | async-start | bytes 589824 | tf_op jit(solution)/shard_map/all_to_all | solution.py:24
  102.6 0.0 all-gather.6.cloned.1.call-start
  102.6 16.4 %all-to-all-done.3 = bf16[4,24,1536]{2,1,0:T(8,128)(2,1)S(1)} async-done(((bf16[4,24,1536]{2,1,0:T(8,128)(2,1)}), bf16[4,24,1536]{2,1,0:T(8,128)(2,1)S(1)}, u32[]{:S(2)}, u32[]{:S(2)}) %all-to-all-start.3) | async-done | bytes 294944 | tf_op jit(solution)/shard_map/all_to_all | solution.py:24
  119.0 1.8 copy-done
  120.9 1.5 copy-done.2
  122.3 1.6 shard_map.68
  124.0 0.0 all-gather.6.cloned.1.call-update
  124.0 12.3 %all_to_all.81 = bf16[8,48,384]{2,1,0:T(8,128)(2,1)S(1)} all-to-all(bf16[8,48,384]{2,1,0:T(8,128)(2,1)S(1)} %bitcast.24), channel_id=1, replica_groups=mesh['z_lo'=4,'y'=4,'core'=2,'x'=4,'z_hi'=4] {'y','core'}, dimensions={0} | all-to-all | bytes 589824 | tf_op jit(solution)/shard_map/all_to_all | solution.py:24
  136.4 12.2 %all_to_all.82 = bf16[4,48,384]{2,1,0:T(8,128)(2,1)S(1)} all-to-all(bf16[4,48,384]{2,1,0:T(8,128)(2,1)S(1)} %broadcast_in_dim.16), channel_id=1, replica_groups=mesh['z_lo'=4,'y'=4,'core'=2,'x'=4,'z_hi'=4] {'z_lo'}, dimensions={0} | all-to-all | bytes 294912 | tf_op jit(solution)/shard_map/all_to_all | solution.py:24
  148.6 10.3 %all_to_all.83 = bf16[8,48,384]{2,1,0:T(8,128)(2,1)S(1)} all-to-all(bf16[8,48,384]{2,1,0:T(8,128)(2,1)S(1)} %broadcast_in_dim.17), channel_id=1, replica_groups=mesh['z_lo'=4,'y'=4,'core'=2,'x'=4,'z_hi'=4] {'y','core'}, dimensions={0} | all-to-all | bytes 589824 | tf_op jit(solution)/shard_map/all_to_all | solution.py:24
  158.9 0.0 copy-done.1
  158.9 0.8 shard_map.69
  159.7 19.4 %all_to_all.84 = bf16[4,24,768]{2,1,0:T(8,128)(2,1)S(1)} all-to-all(bf16[4,24,768]{2,1,0:T(8,128)(2,1)S(1)} %bitcast.23), channel_id=1, replica_groups=mesh['z_lo'=4,'y'=4,'core'=2,'x'=4,'z_hi'=4] {'z_hi'}, dimensions={0} | all-to-all | bytes 294912 | tf_op jit(solution)/shard_map/all_to_all | solution.py:24
  179.1 0.0 copy-done.4
  179.1 0.1 multiply_convert_fusion
  179.2 16.9 %all_to_all.85 = bf16[4,24,768]{2,1,0:T(8,128)(2,1)S(1)} all-to-all(bf16[4,24,768]{2,1,0:T(8,128)(2,1)S(1)} %broadcast_in_dim.18), channel_id=1, replica_groups=mesh['z_lo'=4,'y'=4,'core'=2,'x'=4,'z_hi'=4] {'z_hi'}, dimensions={0} | all-to-all | bytes 294912 | tf_op jit(solution)/shard_map/all_to_all | solution.py:24
  196.1 0.1 pad_maximum_fusion
  196.1 0.0 copy-start.7
  196.2 14.9 %all_to_all.86 = bf16[4,96,1152]{2,1,0:T(8,128)(2,1)S(1)} all-to-all(bf16[4,96,1152]{2,1,0:T(8,128)(2,1)S(1)} %pad_maximum_fusion), channel_id=1, replica_groups=mesh['z_lo'=4,'y'=4,'core'=2,'x'=4,'z_hi'=4] {'x'}, dimensions={0} | all-to-all | bytes 1769472 | tf_op jit(solution)/shard_map/all_to_all | solution.py:24
  211.1 0.6 fusion.2
  211.7 0.7 copy-done.9
  212.3 1.4 fusion.1
  213.7 1.1 copy.9
  (23 shorter events, 0.3 us)
Async XLA Ops:
  7.2 1.9 copy-start.8
  7.2 95.4 %all-gather.8.cloned.1.call-start = ((), (), s32[]{:S(2)}) async-start(), calls=%async_computation.11 | async-start | bytes 2211840 | tf_op jit(solution)/shard_map/all_gather | solution.py:85
  9.0 21.1 %copy-start.10 = (bf16[384,768]{1,0:T(8,128)(2,1)S(1)}, bf16[384,768]{1,0:T(8,128)(2,1)}, u32[]{:S(2)}) copy-start(bf16[384,768]{1,0:T(8,128)(2,1)} %param.7) | copy-start | bytes 1769476
  9.0 21.1 %copy-start.11 = (bf16[384,768]{1,0:T(8,128)(2,1)S(1)}, bf16[384,768]{1,0:T(8,128)(2,1)}, u32[]{:S(2)}) copy-start(bf16[384,768]{1,0:T(8,128)(2,1)} %param.6) | copy-start | bytes 1769476
  30.2 1.8 copy-start.6
  32.0 4.4 %slice-start = ((bf16[768,384]{1,0:T(8,128)(2,1)}), bf16[192,384]{1,0:T(8,128)(2,1)S(1)}, s32[]{:S(2)}) async-start(bf16[768,384]{1,0:T(8,128)(2,1)} %param.9), calls=%async_computation.13 | async-start | bytes 294912 | tf_op jit(solution)/shard_map/slice | solution.py:90
  32.0 4.4 %copy-start.5 = (bf16[768,384]{1,0:T(8,128)(2,1)S(1)}, bf16[768,384]{1,0:T(8,128)(2,1)}, u32[]{:S(2)}) copy-start(bf16[768,384]{1,0:T(8,128)(2,1)} %param.8) | copy-start | bytes 1769476
  32.0 31.4 %all-to-all-start.1 = ((bf16[4,96,1536]{2,1,0:T(8,128)(2,1)}), bf16[4,96,1536]{2,1,0:T(8,128)(2,1)S(1)}, u32[]{:S(2)}, u32[]{:S(2)}) async-start(bf16[4,96,1536]{2,1,0:T(8,128)(2,1)} %bitcast.1), calls=%async_computation.1 | async-start | bytes 2359296 | tf_op jit(solution)/shard_map/all_to_all | solution.py:24
  36.4 82.6 %all-gather.10.cloned.1.call-start = ((), (), s32[]{:S(2)}) async-start(), calls=%async_computation.12 | async-start | bytes 3686400 | tf_op jit(solution)/shard_map/all_gather | solution.py:93
  96.4 0.7 copy-start.3
  97.9 21.1 %all-to-all-start.3 = ((bf16[4,24,1536]{2,1,0:T(8,128)(2,1)}), bf16[4,24,1536]{2,1,0:T(8,128)(2,1)S(1)}, u32[]{:S(2)}, u32[]{:S(2)}) async-start(bf16[4,24,1536]{2,1,0:T(8,128)(2,1)} %broadcast_in_dim.15), calls=%async_computation.3 | async-start | bytes 589824 | tf_op jit(solution)/shard_map/all_to_all | solution.py:24
  102.6 56.3 %all-gather.6.cloned.1.call-start = ((), (), s32[]{:S(2)}) async-start(), calls=%async_computation.10 | async-start | bytes 1474560 | tf_op jit(solution)/shard_map/all_gather | solution.py:107
  119.0 1.8 copy-start
  120.9 1.5 copy-start.2
  122.3 36.5 %copy-start.1 = (bf16[3840,384]{1,0:T(8,128)(2,1)S(1)}, bf16[3840,384]{1,0:T(8,128)(2,1)}, u32[]{:S(2)}) copy-start(bf16[3840,384]{1,0:T(8,128)(2,1)} %all-gather.10.cloned.1.call-done) | copy-start | bytes 8847364
  158.9 20.2 %copy-start.4 = (f32[24,1536]{1,0:T(8,128)S(1)}, f32[24,1536]{1,0:T(8,128)}, u32[]{:S(2)}) copy-start(f32[24,1536]{1,0:T(8,128)} %copy-done.3) | copy-start | bytes 442372
  196.1 14.9 %copy-start.7 = (bf16[384,384]{1,0:T(8,128)(2,1)S(1)}, bf16[384,384]{1,0:T(8,128)(2,1)}, u32[]{:S(2)}) copy-start(bf16[384,384]{1,0:T(8,128)(2,1)} %copy-done.6) | copy-start | bytes 884740
  211.1 1.3 copy-start.9
Sparse Core Ops, SparseCore 0:
  10.7 49.0 all-gather.7
  63.8 45.3 all-gather.9
  124.1 26.5 all-gather.5

commit v5 on v1

--- a/solution.py
+++ b/solution.py
@@ -31,6 +31,11 @@
     return swap(jnp.broadcast_to(block[None], (count,) + block.shape).reshape(-1, block.shape[1]), axes)
 
 
+def exchange_sum(partial, axes, count):
+    arrived = gather(partial.astype(bf16), axes, count)
+    return jnp.sum(arrived.reshape((count,) + partial.shape).astype(f32), axis=0)
+
+
 def scatter_sum_col(partial):
     return scatter_sum(scatter_sum(partial, "x", 4), "z_hi", 4)
 
@@ -60,7 +65,8 @@
     acts = gather_col(jnp.concatenate([own_activation, own_tangent], axis=1))
     activation, tangent_act = acts[:, :width], acts[:, width:]
     partial_out = dot(tangent_act, second_weight, 1, 0) + dot(activation, second_tangent, 1, 0)
-    tangent_out = gather(scatter_sum(partial_out, ROW, 32).astype(bf16), ROW, 32)
+    out_share = exchange_sum(scatter_sum(partial_out, ("y", "core"), 8), "z_lo", 4).astype(bf16)
+    tangent_out = gather(out_share, ("y", "core"), 8)
     grad_act = scatter_sum_col(dot(tangent_out, second_weight, 1, 1))
     grad_pre = gather_col((grad_act * derivative).astype(bf16))
     scaling = 1.0 / math.sqrt(token_count)

time: 223 us -> 216 us (0.969)
  the two profiles are of different devices: /device:TPU:32 before, /device:TPU:2 now
where the time goes in v5:
time: 216 us; the launch traced here: 215 us
  blocking collectives  196 us (91%)
  waiting for transfers between devices  5.59 us (3%)
  starting transfers between devices  4.9 us (2%)
  matrix products  4.16 us (2%)
  local copies, waits for them, and re-layouts  3.63 us (2%)
    all_to_all x11, blocking collectives, swap(): return lax.all_to_all(blocks, axes, 0, 0, tiled=True)  196 us
    all_to_all x1, waiting for transfers between devices, swap(): return lax.all_to_all(blocks, axes, 0, 0, tiled=True)  5.59 us
    all_to_all x1, starting transfers between devices, swap(): return lax.all_to_all(blocks, axes, 0, 0, tiled=True)  4.9 us
  transfers between devices with their start and end apart: 1, of which 1 were waited for; matrix products, arithmetic and copies ran while one was open for 1% of the time, Pallas kernels for 0%

profile of v5, /device:TPU:2, one launch (start us, length us, event | category | flops | bytes accessed | tf_op | source)
XLA Modules:
  0.0 215.3 jit_solution(1262307974878370709)
XLA Ops:
  0.6 0.0 copy-start
  0.6 0.0 copy-start.2
  0.7 0.0 copy-start.3
  0.7 0.9 broadcast_in_dim.18
  1.5 22.2 %all_to_all.99 = bf16[32,12,384]{2,1,0:T(8,128)(2,1)S(1)} all-to-all(bf16[32,12,384]{2,1,0:T(8,128)(2,1)S(1)} %broadcast_in_dim.18), channel_id=1, replica_groups=mesh['z_lo'=4,'y'=4,'core'=2,'x'=4,'z_hi'=4] {'z_lo','y','core'}, dimensions={0} | all-to-all | bytes 589824 | tf_op jit(solution)/shard_map/all_to_all | solution.py:22
  23.8 0.1 all_to_all.67
  23.8 0.0 copy-done.2
  23.8 0.0 copy-done.3
  23.9 0.8 convolution_convert_fusion
  24.6 20.4 %all_to_all.100 = bf16[4,96,1536]{2,1,0:T(8,128)(2,1)S(1)} all-to-all(bf16[4,96,1536]{2,1,0:T(8,128)(2,1)S(1)} %bitcast.26), channel_id=1, replica_groups=mesh['z_lo'=4,'y'=4,'core'=2,'x'=4,'z_hi'=4] {'x'}, dimensions={0} | all-to-all | bytes 2359296 | tf_op jit(solution)/shard_map/all_to_all | solution.py:22
  45.0 0.2 reduce_sum.66
  45.2 32.5 %all_to_all.101 = bf16[4,24,1536]{2,1,0:T(8,128)(2,1)S(1)} all-to-all(bf16[4,24,1536]{2,1,0:T(8,128)(2,1)S(1)} %bitcast.29), channel_id=1, replica_groups=mesh['z_lo'=4,'y'=4,'core'=2,'x'=4,'z_hi'=4] {'z_hi'}, dimensions={0} | all-to-all | bytes 589824 | tf_op jit(solution)/shard_map/all_to_all | solution.py:22
  77.7 0.1 multiply_convert_fusion.1
  77.8 23.4 %all_to_all.102 = bf16[4,24,1536]{2,1,0:T(8,128)(2,1)S(1)} all-to-all(bf16[4,24,1536]{2,1,0:T(8,128)(2,1)S(1)} %broadcast_in_dim.19), channel_id=1, replica_groups=mesh['z_lo'=4,'y'=4,'core'=2,'x'=4,'z_hi'=4] {'z_hi'}, dimensions={0} | all-to-all | bytes 589824 | tf_op jit(solution)/shard_map/all_to_all | solution.py:22
  101.2 0.1 broadcast_in_dim.21
  101.3 15.5 %all_to_all.103 = bf16[4,96,1536]{2,1,0:T(8,128)(2,1)S(1)} all-to-all(bf16[4,96,1536]{2,1,0:T(8,128)(2,1)S(1)} %broadcast_in_dim.21), channel_id=1, replica_groups=mesh['z_lo'=4,'y'=4,'core'=2,'x'=4,'z_hi'=4] {'x'}, dimensions={0} | all-to-all | bytes 2359296 | tf_op jit(solution)/shard_map/all_to_all | solution.py:22
  116.8 0.0 copy-start.1
  116.8 0.0 copy-done
  116.8 0.5 fusion.7
  117.3 0.6 copy-done.1
  117.8 0.5 fusion.3
  118.3 10.3 %all_to_all.104 = bf16[8,48,384]{2,1,0:T(8,128)(2,1)S(1)} all-to-all(bf16[8,48,384]{2,1,0:T(8,128)(2,1)S(1)} %bitcast.31), channel_id=1, replica_groups=mesh['z_lo'=4,'y'=4,'core'=2,'x'=4,'z_hi'=4] {'y','core'}, dimensions={0} | all-to-all | bytes 589824 | tf_op jit(solution)/shard_map/all_to_all | solution.py:22
  128.7 12.2 %all_to_all.105 = bf16[4,48,384]{2,1,0:T(8,128)(2,1)S(1)} all-to-all(bf16[4,48,384]{2,1,0:T(8,128)(2,1)S(1)} %broadcast_in_dim.22), channel_id=1, replica_groups=mesh['z_lo'=4,'y'=4,'core'=2,'x'=4,'z_hi'=4] {'z_lo'}, dimensions={0} | all-to-all | bytes 294912 | tf_op jit(solution)/shard_map/all_to_all | solution.py:22
  141.0 10.3 %all_to_all.106 = bf16[8,48,384]{2,1,0:T(8,128)(2,1)S(1)} all-to-all(bf16[8,48,384]{2,1,0:T(8,128)(2,1)S(1)} %broadcast_in_dim.23), channel_id=1, replica_groups=mesh['z_lo'=4,'y'=4,'core'=2,'x'=4,'z_hi'=4] {'y','core'}, dimensions={0} | all-to-all | bytes 589824 | tf_op jit(solution)/shard_map/all_to_all | solution.py:22
  151.2 0.5 convolution_convert_fusion.1
  151.7 12.9 %all_to_all.107 = bf16[4,96,768]{2,1,0:T(8,128)(2,1)S(1)} all-to-all(bf16[4,96,768]{2,1,0:T(8,128)(2,1)S(1)} %bitcast.25), channel_id=1, replica_groups=mesh['z_lo'=4,'y'=4,'core'=2,'x'=4,'z_hi'=4] {'x'}, dimensions={0} | all-to-all | bytes 1179648 | tf_op jit(solution)/shard_map/all_to_all | solution.py:22
  164.7 0.1 reduce_sum.70
  164.8 18.3 %all_to_all.108 = bf16[4,24,768]{2,1,0:T(8,128)(2,1)S(1)} all-to-all(bf16[4,24,768]{2,1,0:T(8,128)(2,1)S(1)} %bitcast.32), channel_id=1, replica_groups=mesh['z_lo'=4,'y'=4,'core'=2,'x'=4,'z_hi'=4] {'z_hi'}, dimensions={0} | all-to-all | bytes 294912 | tf_op jit(solution)/shard_map/all_to_all | solution.py:22
  183.1 0.1 multiply_convert_fusion
  183.2 17.7 %all_to_all.109 = bf16[4,24,768]{2,1,0:T(8,128)(2,1)S(1)} all-to-all(bf16[4,24,768]{2,1,0:T(8,128)(2,1)S(1)} %broadcast_in_dim.24), channel_id=1, replica_groups=mesh['z_lo'=4,'y'=4,'core'=2,'x'=4,'z_hi'=4] {'z_hi'}, dimensions={0} | all-to-all | bytes 294912 | tf_op jit(solution)/shard_map/all_to_all | solution.py:22
  200.9 0.9 broadcast_in_dim.26
  201.7 4.9 %all-to-all-start.11 = ((bf16[4,96,768]{2,1,0:T(8,128)(2,1)}), bf16[4,96,768]{2,1,0:T(8,128)(2,1)S(1)}, u32[]{:S(2)}, u32[]{:S(2)}) async-start(bf16[4,96,768]{2,1,0:T(8,128)(2,1)} %broadcast_in_dim.26), calls=%async_computation.11 | async-start | bytes 1179648 | tf_op jit(solution)/shard_map/all_to_all | solution.py:22
  206.7 1.4 fusion.1
  208.0 5.6 %all-to-all-done.11 = bf16[4,96,768]{2,1,0:T(8,128)(2,1)S(1)} async-done(((bf16[4,96,768]{2,1,0:T(8,128)(2,1)}), bf16[4,96,768]{2,1,0:T(8,128)(2,1)S(1)}, u32[]{:S(2)}, u32[]{:S(2)}) %all-to-all-start.11) | async-done | bytes 589856 | tf_op jit(solution)/shard_map/all_to_all | solution.py:22
  213.6 0.6 fusion.2
  214.2 1.1 copy.9
  (9 shorter events, 0.2 us)
Async XLA Ops:
  0.6 116.2 %copy-start = (bf16[768,384]{1,0:T(8,128)(2,1)S(1)}, bf16[768,384]{1,0:T(8,128)(2,1)}, u32[]{:S(2)}) copy-start(bf16[768,384]{1,0:T(8,128)(2,1)} %param.8) | copy-start | bytes 1769476
  0.6 23.2 %copy-start.2 = (bf16[384,768]{1,0:T(8,128)(2,1)S(1)}, bf16[384,768]{1,0:T(8,128)(2,1)}, u32[]{:S(2)}) copy-start(bf16[384,768]{1,0:T(8,128)(2,1)} %param.7) | copy-start | bytes 1769476
  0.7 23.2 %copy-start.3 = (bf16[384,768]{1,0:T(8,128)(2,1)S(1)}, bf16[384,768]{1,0:T(8,128)(2,1)}, u32[]{:S(2)}) copy-start(bf16[384,768]{1,0:T(8,128)(2,1)} %param.6) | copy-start | bytes 1769476
  116.8 1.1 copy-start.1
  201.7 11.9 %all-to-all-start.11 = ((bf16[4,96,768]{2,1,0:T(8,128)(2,1)}), bf16[4,96,768]{2,1,0:T(8,128)(2,1)S(1)}, u32[]{:S(2)}, u32[]{:S(2)}) async-start(bf16[4,96,768]{2,1,0:T(8,128)(2,1)} %broadcast_in_dim.26), calls=%async_computation.11 | async-start | bytes 1179648 | tf_op jit(solution)/shard_map/all_to_all | solution.py:22

commit v6 on v5

--- a/solution.py
+++ b/solution.py
@@ -3,6 +3,8 @@
 import jax
 import jax.numpy as jnp
 from jax import lax
+from jax.experimental import pallas as pl
+from jax.experimental.pallas import tpu as pltpu
 from jax.sharding import Mesh, PartitionSpec as P
 
 sqrt_two_pi = 0.7978845608028654
@@ -55,16 +57,27 @@
     return (activation, derivative, tangent_act)
 
 
+def out_kernel(acts_ref, weight_ref, tangent_ref, out_ref):
+    width = weight_ref.shape[0]
+    total = dot(acts_ref[:, width:], weight_ref[...], 1, 0)
+    out_ref[...] = (total + dot(acts_ref[:, :width], tangent_ref[...], 1, 0)).astype(bf16)
+
+
+def call(kernel, *shape, **rest):
+    params = pltpu.CompilerParams(vmem_limit_bytes=16 * 1024 * 1024)
+    return pl.pallas_call(kernel, out_shape=jax.ShapeDtypeStruct(shape, bf16), compiler_params=params, **rest)
+
+
 def shards(tokens, first_weight, first_tangent, second_weight, second_tangent):
-    gathered = gather(tokens, ROW, 32)
+    gathered = gather(gather(tokens, ("y", "core"), 8), "z_lo", 4)
     token_count = gathered.shape[0]
     width = first_weight.shape[1]
     joined = jnp.concatenate([first_weight, first_tangent], axis=1)
     summed = scatter_sum_col(dot(gathered, joined, 1, 0))
     own_activation, derivative, own_tangent = activate(summed[:, :width], summed[:, width:])
     acts = gather_col(jnp.concatenate([own_activation, own_tangent], axis=1))
-    activation, tangent_act = acts[:, :width], acts[:, width:]
-    partial_out = dot(tangent_act, second_weight, 1, 0) + dot(activation, second_tangent, 1, 0)
+    activation = acts[:, :width]
+    partial_out = call(out_kernel, token_count, second_weight.shape[1])(acts, second_weight, second_tangent)
     out_share = exchange_sum(scatter_sum(partial_out, ("y", "core"), 8), "z_lo", 4).astype(bf16)
     tangent_out = gather(out_share, ("y", "core"), 8)
     grad_act = scatter_sum_col(dot(tangent_out, second_weight, 1, 1))

time: 216 us -> 211 us (0.977)
  blocking collectives: 196 us -> 191 us
    all_to_all x11 -> x12, blocking collectives: 196 us -> 191 us  [swap(): return lax.all_to_all(blocks, axes, 0, 0, tiled=True)]
where the time goes in v6:
time: 211 us; the launch traced here: 210 us
  blocking collectives  191 us (91%)
  waiting for transfers between devices  5.59 us (3%)
  starting transfers between devices  4.9 us (2%)
  matrix products  3.23 us (2%)
  local copies, waits for them, and re-layouts  2.97 us (1%)
    all_to_all x12, blocking collectives, swap(): return lax.all_to_all(blocks, axes, 0, 0, tiled=True)  191 us
    all_to_all x1, waiting for transfers between devices, swap(): return lax.all_to_all(blocks, axes, 0, 0, tiled=True)  5.59 us
    all_to_all x1, starting transfers between devices, swap(): return lax.all_to_all(blocks, axes, 0, 0, tiled=True)  4.9 us
  transfers between devices with their start and end apart: 1, of which 1 were waited for; matrix products, arithmetic and copies ran while one was open for 1% of the time, Pallas kernels for 0%

profile of v6, /device:TPU:2, one launch (start us, length us, event | category | flops | bytes accessed | tf_op | source)
XLA Modules:
  0.0 210.0 jit_solution(1526927685315416083)
XLA Ops:
  0.6 0.0 copy-start.2
  0.6 0.0 copy-start.3
  0.6 0.8 broadcast_in_dim.22
  1.5 10.1 %all_to_all.101 = bf16[8,12,384]{2,1,0:T(8,128)(2,1)S(1)} all-to-all(bf16[8,12,384]{2,1,0:T(8,128)(2,1)S(1)} %broadcast_in_dim.22), channel_id=1, replica_groups=mesh['z_lo'=4,'y'=4,'core'=2,'x'=4,'z_hi'=4] {'y','core'}, dimensions={0} | all-to-all | bytes 147456 | tf_op jit(solution)/shard_map/all_to_all | solution.py:24
  11.6 15.1 %all_to_all.102 = bf16[4,96,384]{2,1,0:T(8,128)(2,1)S(1)} all-to-all(bf16[4,96,384]{2,1,0:T(8,128)(2,1)S(1)} %broadcast_in_dim.24), channel_id=1, replica_groups=mesh['z_lo'=4,'y'=4,'core'=2,'x'=4,'z_hi'=4] {'z_lo'}, dimensions={0} | all-to-all | bytes 589824 | tf_op jit(solution)/shard_map/all_to_all | solution.py:24
  26.7 0.0 copy-done.2
  26.7 0.0 copy-done.3
  26.7 0.8 convolution_convert_fusion
  27.5 17.4 %all_to_all.103 = bf16[4,96,1536]{2,1,0:T(8,128)(2,1)S(1)} all-to-all(bf16[4,96,1536]{2,1,0:T(8,128)(2,1)S(1)} %bitcast.32), channel_id=1, replica_groups=mesh['z_lo'=4,'y'=4,'core'=2,'x'=4,'z_hi'=4] {'x'}, dimensions={0} | all-to-all | bytes 2359296 | tf_op jit(solution)/shard_map/all_to_all | solution.py:24
  44.9 0.2 reduce_sum.66
  45.1 30.1 %all_to_all.104 = bf16[4,24,1536]{2,1,0:T(8,128)(2,1)S(1)} all-to-all(bf16[4,24,1536]{2,1,0:T(8,128)(2,1)S(1)} %bitcast.35), channel_id=1, replica_groups=mesh['z_lo'=4,'y'=4,'core'=2,'x'=4,'z_hi'=4] {'z_hi'}, dimensions={0} | all-to-all | bytes 589824 | tf_op jit(solution)/shard_map/all_to_all | solution.py:24
  75.3 0.1 multiply_convert_fusion.1
  75.4 21.7 %all_to_all.105 = bf16[4,24,1536]{2,1,0:T(8,128)(2,1)S(1)} all-to-all(bf16[4,24,1536]{2,1,0:T(8,128)(2,1)S(1)} %broadcast_in_dim.25), channel_id=1, replica_groups=mesh['z_lo'=4,'y'=4,'core'=2,'x'=4,'z_hi'=4] {'z_hi'}, dimensions={0} | all-to-all | bytes 589824 | tf_op jit(solution)/shard_map/all_to_all | solution.py:24
  97.1 0.1 broadcast_in_dim.27
  97.2 0.0 copy-start
  97.2 0.0 copy-start.1
  97.2 14.2 %all_to_all.106 = bf16[4,96,1536]{2,1,0:T(8,128)(2,1)S(1)} all-to-all(bf16[4,96,1536]{2,1,0:T(8,128)(2,1)S(1)} %broadcast_in_dim.27), channel_id=1, replica_groups=mesh['z_lo'=4,'y'=4,'core'=2,'x'=4,'z_hi'=4] {'x'}, dimensions={0} | all-to-all | bytes 2359296 | tf_op jit(solution)/shard_map/all_to_all | solution.py:24
  111.4 0.0 copy-done
  111.4 0.0 copy-done.1
  111.4 0.8 shard_map.68
  112.2 10.3 %all_to_all.107 = bf16[8,48,384]{2,1,0:T(8,128)(2,1)S(1)} all-to-all(bf16[8,48,384]{2,1,0:T(8,128)(2,1)S(1)} %bitcast.30), channel_id=1, replica_groups=mesh['z_lo'=4,'y'=4,'core'=2,'x'=4,'z_hi'=4] {'y','core'}, dimensions={0} | all-to-all | bytes 589824 | tf_op jit(solution)/shard_map/all_to_all | solution.py:24
  122.5 13.5 %all_to_all.108 = bf16[4,48,384]{2,1,0:T(8,128)(2,1)S(1)} all-to-all(bf16[4,48,384]{2,1,0:T(8,128)(2,1)S(1)} %broadcast_in_dim.28), channel_id=1, replica_groups=mesh['z_lo'=4,'y'=4,'core'=2,'x'=4,'z_hi'=4] {'z_lo'}, dimensions={0} | all-to-all | bytes 294912 | tf_op jit(solution)/shard_map/all_to_all | solution.py:24
  136.1 10.3 %all_to_all.109 = bf16[8,48,384]{2,1,0:T(8,128)(2,1)S(1)} all-to-all(bf16[8,48,384]{2,1,0:T(8,128)(2,1)S(1)} %broadcast_in_dim.29), channel_id=1, replica_groups=mesh['z_lo'=4,'y'=4,'core'=2,'x'=4,'z_hi'=4] {'y','core'}, dimensions={0} | all-to-all | bytes 589824 | tf_op jit(solution)/shard_map/all_to_all | solution.py:24
  146.4 0.5 convolution_convert_fusion.1
  146.9 12.9 %all_to_all.110 = bf16[4,96,768]{2,1,0:T(8,128)(2,1)S(1)} all-to-all(bf16[4,96,768]{2,1,0:T(8,128)(2,1)S(1)} %bitcast.31), channel_id=1, replica_groups=mesh['z_lo'=4,'y'=4,'core'=2,'x'=4,'z_hi'=4] {'x'}, dimensions={0} | all-to-all | bytes 1179648 | tf_op jit(solution)/shard_map/all_to_all | solution.py:24
  159.8 0.1 reduce_sum.70
  159.9 17.8 %all_to_all.111 = bf16[4,24,768]{2,1,0:T(8,128)(2,1)S(1)} all-to-all(bf16[4,24,768]{2,1,0:T(8,128)(2,1)S(1)} %bitcast.37), channel_id=1, replica_groups=mesh['z_lo'=4,'y'=4,'core'=2,'x'=4,'z_hi'=4] {'z_hi'}, dimensions={0} | all-to-all | bytes 294912 | tf_op jit(solution)/shard_map/all_to_all | solution.py:24
  177.8 0.1 multiply_convert_fusion
  177.8 17.7 %all_to_all.112 = bf16[4,24,768]{2,1,0:T(8,128)(2,1)S(1)} all-to-all(bf16[4,24,768]{2,1,0:T(8,128)(2,1)S(1)} %broadcast_in_dim.30), channel_id=1, replica_groups=mesh['z_lo'=4,'y'=4,'core'=2,'x'=4,'z_hi'=4] {'z_hi'}, dimensions={0} | all-to-all | bytes 294912 | tf_op jit(solution)/shard_map/all_to_all | solution.py:24
  195.6 0.9 broadcast_in_dim.64
  196.4 4.9 %all-to-all-start.12 = ((bf16[4,96,768]{2,1,0:T(8,128)(2,1)}), bf16[4,96,768]{2,1,0:T(8,128)(2,1)S(1)}, u32[]{:S(2)}, u32[]{:S(2)}) async-start(bf16[4,96,768]{2,1,0:T(8,128)(2,1)} %broadcast_in_dim.64), calls=%async_computation.12 | async-start | bytes 1179648 | tf_op jit(solution)/shard_map/all_to_all | solution.py:24
  201.3 1.4 fusion.2
  202.7 5.6 %all-to-all-done.12 = bf16[4,96,768]{2,1,0:T(8,128)(2,1)S(1)} async-done(((bf16[4,96,768]{2,1,0:T(8,128)(2,1)}), bf16[4,96,768]{2,1,0:T(8,128)(2,1)S(1)}, u32[]{:S(2)}, u32[]{:S(2)}) %all-to-all-start.12) | async-done | bytes 589856 | tf_op jit(solution)/shard_map/all_to_all | solution.py:24
  208.3 0.6 fusion.3
  208.9 1.1 copy.9
  (11 shorter events, 0.3 us)
Async XLA Ops:
  0.6 26.1 %copy-start.2 = (bf16[384,768]{1,0:T(8,128)(2,1)S(1)}, bf16[384,768]{1,0:T(8,128)(2,1)}, u32[]{:S(2)}) copy-start(bf16[384,768]{1,0:T(8,128)(2,1)} %param.7) | copy-start | bytes 1769476
  0.6 26.1 %copy-start.3 = (bf16[384,768]{1,0:T(8,128)(2,1)S(1)}, bf16[384,768]{1,0:T(8,128)(2,1)}, u32[]{:S(2)}) copy-start(bf16[384,768]{1,0:T(8,128)(2,1)} %param.6) | copy-start | bytes 1769476
  97.2 14.2 %copy-start = (bf16[768,384]{1,0:T(8,128)(2,1)S(1)}, bf16[768,384]{1,0:T(8,128)(2,1)}, u32[]{:S(2)}) copy-start(bf16[768,384]{1,0:T(8,128)(2,1)} %weight_ref.1) | copy-start | bytes 1769476
  97.2 14.2 %copy-start.1 = (bf16[768,384]{1,0:T(8,128)(2,1)S(1)}, bf16[768,384]{1,0:T(8,128)(2,1)}, u32[]{:S(2)}) copy-start(bf16[768,384]{1,0:T(8,128)(2,1)} %tangent_ref.1) | copy-start | bytes 1769476
  196.4 11.9 %all-to-all-start.12 = ((bf16[4,96,768]{2,1,0:T(8,128)(2,1)}), bf16[4,96,768]{2,1,0:T(8,128)(2,1)S(1)}, u32[]{:S(2)}, u32[]{:S(2)}) async-start(bf16[4,96,768]{2,1,0:T(8,128)(2,1)} %broadcast_in_dim.64), calls=%async_computation.12 | async-start | bytes 1179648 | tf_op jit(solution)/shard_map/all_to_all | solution.py:24

commit v7 on v6

--- a/solution.py
+++ b/solution.py
@@ -1,3 +1,4 @@
+import functools
 import math
 
 import jax
@@ -57,6 +58,12 @@
     return (activation, derivative, tangent_act)
 
 
+def last_kernel(scaling, tokens_ref, grad_ref, acts_ref, outs_ref, first_ref, second_ref):
+    width = second_ref.shape[0]
+    second_ref[...] = (dot(acts_ref[:, :width], outs_ref[...], 0, 0) * scaling).astype(bf16)
+    first_ref[...] = (dot(tokens_ref[...], grad_ref[...], 0, 0) * scaling).astype(bf16)
+
+
 def out_kernel(acts_ref, weight_ref, tangent_ref, out_ref):
     width = weight_ref.shape[0]
     total = dot(acts_ref[:, width:], weight_ref[...], 1, 0)
@@ -76,16 +83,20 @@
     summed = scatter_sum_col(dot(gathered, joined, 1, 0))
     own_activation, derivative, own_tangent = activate(summed[:, :width], summed[:, width:])
     acts = gather_col(jnp.concatenate([own_activation, own_tangent], axis=1))
-    activation = acts[:, :width]
     partial_out = call(out_kernel, token_count, second_weight.shape[1])(acts, second_weight, second_tangent)
     out_share = exchange_sum(scatter_sum(partial_out, ("y", "core"), 8), "z_lo", 4).astype(bf16)
     tangent_out = gather(out_share, ("y", "core"), 8)
     grad_act = scatter_sum_col(dot(tangent_out, second_weight, 1, 1))
     grad_pre = gather_col((grad_act * derivative).astype(bf16))
     scaling = 1.0 / math.sqrt(token_count)
-    first_curvature = (dot(gathered, grad_pre, 0, 0) * scaling).astype(bf16)
-    second_curvature = (dot(activation, tangent_out, 0, 0) * scaling).astype(bf16)
-    return (first_curvature, second_curvature)
+    features = gathered.shape[1]
+    first_shape = jax.ShapeDtypeStruct((features, width), bf16)
+    second_shape = jax.ShapeDtypeStruct((width, features), bf16)
+    return pl.pallas_call(
+        functools.partial(last_kernel, scaling),
+        out_shape=(first_shape, second_shape),
+        compiler_params=pltpu.CompilerParams(vmem_limit_bytes=16 * 1024 * 1024),
+    )(gathered, grad_pre, acts, tangent_out)
 
 
 def solution(mesh):

time: 211 us -> 209 us (level)
  blocking collectives: 191 us -> 202 us
  waiting for transfers between devices: 5.59 us -> 0 us
  starting transfers between devices: 4.9 us -> 0 us
    all_to_all x12 -> x13, blocking collectives: 191 us -> 202 us  [swap(): return lax.all_to_all(blocks, axes, 0, 0, tiled=True)]
    all_to_all x1 -> x0, waiting for transfers between devices: 5.59 us -> none  [swap(): return lax.all_to_all(blocks, axes, 0, 0, tiled=True)]
    all_to_all x1 -> x0, starting transfers between devices: 4.9 us -> none  [swap(): return lax.all_to_all(blocks, axes, 0, 0, tiled=True)]
  transfers between devices with their start and end apart: 1 -> 0, of which waited for: 1 -> 0; matrix products, arithmetic and copies ran while one was open for 1% -> 0% of each run, Pallas kernels for 0% -> 0%
where the time goes in v7:
time: 209 us; the launch traced here: 208 us
  blocking collectives  202 us (97%)
  Pallas kernels  2.47 us (1%)
    all_to_all x13, blocking collectives, swap(): return lax.all_to_all(blocks, axes, 0, 0, tiled=True)  202 us

profile of v7, /device:TPU:2, one launch (start us, length us, event | category | flops | bytes accessed | tf_op | source)
XLA Modules:
  0.0 208.1 jit_solution(454616002650118311)
XLA Ops:
  0.6 0.0 copy-start.2
  0.6 0.0 copy-start.3
  0.6 0.8 broadcast_in_dim.22
  1.5 10.1 %all_to_all.101 = bf16[8,12,384]{2,1,0:T(8,128)(2,1)S(1)} all-to-all(bf16[8,12,384]{2,1,0:T(8,128)(2,1)S(1)} %broadcast_in_dim.22), channel_id=1, replica_groups=mesh['z_lo'=4,'y'=4,'core'=2,'x'=4,'z_hi'=4] {'y','core'}, dimensions={0} | all-to-all | bytes 147456 | tf_op jit(solution)/shard_map/all_to_all | solution.py:25
  11.6 15.1 %all_to_all.102 = bf16[4,96,384]{2,1,0:T(8,128)(2,1)S(1)} all-to-all(bf16[4,96,384]{2,1,0:T(8,128)(2,1)S(1)} %broadcast_in_dim.24), channel_id=1, replica_groups=mesh['z_lo'=4,'y'=4,'core'=2,'x'=4,'z_hi'=4] {'z_lo'}, dimensions={0} | all-to-all | bytes 589824 | tf_op jit(solution)/shard_map/all_to_all | solution.py:25
  26.7 0.0 copy-done.2
  26.7 0.0 copy-done.3
  26.7 0.8 convolution_convert_fusion
  27.5 17.4 %all_to_all.103 = bf16[4,96,1536]{2,1,0:T(8,128)(2,1)S(1)} all-to-all(bf16[4,96,1536]{2,1,0:T(8,128)(2,1)S(1)} %bitcast.25), channel_id=1, replica_groups=mesh['z_lo'=4,'y'=4,'core'=2,'x'=4,'z_hi'=4] {'x'}, dimensions={0} | all-to-all | bytes 2359296 | tf_op jit(solution)/shard_map/all_to_all | solution.py:25
  44.9 0.2 reduce_sum.66
  45.1 30.1 %all_to_all.104 = bf16[4,24,1536]{2,1,0:T(8,128)(2,1)S(1)} all-to-all(bf16[4,24,1536]{2,1,0:T(8,128)(2,1)S(1)} %bitcast.26), channel_id=1, replica_groups=mesh['z_lo'=4,'y'=4,'core'=2,'x'=4,'z_hi'=4] {'z_hi'}, dimensions={0} | all-to-all | bytes 589824 | tf_op jit(solution)/shard_map/all_to_all | solution.py:25
  75.3 0.1 multiply_convert_fusion.1
  75.4 21.7 %all_to_all.105 = bf16[4,24,1536]{2,1,0:T(8,128)(2,1)S(1)} all-to-all(bf16[4,24,1536]{2,1,0:T(8,128)(2,1)S(1)} %broadcast_in_dim.25), channel_id=1, replica_groups=mesh['z_lo'=4,'y'=4,'core'=2,'x'=4,'z_hi'=4] {'z_hi'}, dimensions={0} | all-to-all | bytes 589824 | tf_op jit(solution)/shard_map/all_to_all | solution.py:25
  97.1 0.1 broadcast_in_dim.27
  97.2 0.0 copy-start
  97.2 0.0 copy-start.1
  97.2 14.2 %all_to_all.106 = bf16[4,96,1536]{2,1,0:T(8,128)(2,1)S(1)} all-to-all(bf16[4,96,1536]{2,1,0:T(8,128)(2,1)S(1)} %broadcast_in_dim.27), channel_id=1, replica_groups=mesh['z_lo'=4,'y'=4,'core'=2,'x'=4,'z_hi'=4] {'x'}, dimensions={0} | all-to-all | bytes 2359296 | tf_op jit(solution)/shard_map/all_to_all | solution.py:25
  111.4 0.0 copy-done
  111.4 0.0 copy-done.1
  111.4 0.8 shard_map.68
  112.2 10.3 %all_to_all.107 = bf16[8,48,384]{2,1,0:T(8,128)(2,1)S(1)} all-to-all(bf16[8,48,384]{2,1,0:T(8,128)(2,1)S(1)} %bitcast.23), channel_id=1, replica_groups=mesh['z_lo'=4,'y'=4,'core'=2,'x'=4,'z_hi'=4] {'y','core'}, dimensions={0} | all-to-all | bytes 589824 | tf_op jit(solution)/shard_map/all_to_all | solution.py:25
  122.5 13.5 %all_to_all.108 = bf16[4,48,384]{2,1,0:T(8,128)(2,1)S(1)} all-to-all(bf16[4,48,384]{2,1,0:T(8,128)(2,1)S(1)} %broadcast_in_dim.28), channel_id=1, replica_groups=mesh['z_lo'=4,'y'=4,'core'=2,'x'=4,'z_hi'=4] {'z_lo'}, dimensions={0} | all-to-all | bytes 294912 | tf_op jit(solution)/shard_map/all_to_all | solution.py:25
  136.1 10.3 %all_to_all.109 = bf16[8,48,384]{2,1,0:T(8,128)(2,1)S(1)} all-to-all(bf16[8,48,384]{2,1,0:T(8,128)(2,1)S(1)} %broadcast_in_dim.29), channel_id=1, replica_groups=mesh['z_lo'=4,'y'=4,'core'=2,'x'=4,'z_hi'=4] {'y','core'}, dimensions={0} | all-to-all | bytes 589824 | tf_op jit(solution)/shard_map/all_to_all | solution.py:25
  146.4 0.5 convolution_convert_fusion.1
  146.9 12.9 %all_to_all.110 = bf16[4,96,768]{2,1,0:T(8,128)(2,1)S(1)} all-to-all(bf16[4,96,768]{2,1,0:T(8,128)(2,1)S(1)} %bitcast.24), channel_id=1, replica_groups=mesh['z_lo'=4,'y'=4,'core'=2,'x'=4,'z_hi'=4] {'x'}, dimensions={0} | all-to-all | bytes 1179648 | tf_op jit(solution)/shard_map/all_to_all | solution.py:25
  159.8 0.1 reduce_sum.70
  159.9 17.8 %all_to_all.111 = bf16[4,24,768]{2,1,0:T(8,128)(2,1)S(1)} all-to-all(bf16[4,24,768]{2,1,0:T(8,128)(2,1)S(1)} %bitcast.28), channel_id=1, replica_groups=mesh['z_lo'=4,'y'=4,'core'=2,'x'=4,'z_hi'=4] {'z_hi'}, dimensions={0} | all-to-all | bytes 294912 | tf_op jit(solution)/shard_map/all_to_all | solution.py:25
  177.8 0.1 multiply_convert_fusion
  177.8 17.7 %all_to_all.112 = bf16[4,24,768]{2,1,0:T(8,128)(2,1)S(1)} all-to-all(bf16[4,24,768]{2,1,0:T(8,128)(2,1)S(1)} %broadcast_in_dim.30), channel_id=1, replica_groups=mesh['z_lo'=4,'y'=4,'core'=2,'x'=4,'z_hi'=4] {'z_hi'}, dimensions={0} | all-to-all | bytes 294912 | tf_op jit(solution)/shard_map/all_to_all | solution.py:25
  195.6 10.8 %all_to_all.113 = bf16[4,96,768]{2,1,0:T(8,128)(2,1)S(1)} all-to-all(bf16[4,96,768]{2,1,0:T(8,128)(2,1)S(1)} %broadcast_in_dim.64), channel_id=1, replica_groups=mesh['z_lo'=4,'y'=4,'core'=2,'x'=4,'z_hi'=4] {'x'}, dimensions={0} | all-to-all | bytes 1179648 | tf_op jit(solution)/shard_map/all_to_all | solution.py:25
  206.4 1.7 shard_map.69
  (12 shorter events, 0.3 us)
Async XLA Ops:
  0.6 26.1 %copy-start.2 = (bf16[384,768]{1,0:T(8,128)(2,1)S(1)}, bf16[384,768]{1,0:T(8,128)(2,1)}, u32[]{:S(2)}) copy-start(bf16[384,768]{1,0:T(8,128)(2,1)} %param.7) | copy-start | bytes 1769476
  0.6 26.1 %copy-start.3 = (bf16[384,768]{1,0:T(8,128)(2,1)S(1)}, bf16[384,768]{1,0:T(8,128)(2,1)}, u32[]{:S(2)}) copy-start(bf16[384,768]{1,0:T(8,128)(2,1)} %param.6) | copy-start | bytes 1769476
  97.2 14.2 %copy-start = (bf16[768,384]{1,0:T(8,128)(2,1)S(1)}, bf16[768,384]{1,0:T(8,128)(2,1)}, u32[]{:S(2)}) copy-start(bf16[768,384]{1,0:T(8,128)(2,1)} %weight_ref.1) | copy-start | bytes 1769476
  97.2 14.2 %copy-start.1 = (bf16[768,384]{1,0:T(8,128)(2,1)S(1)}, bf16[768,384]{1,0:T(8,128)(2,1)}, u32[]{:S(2)}) copy-start(bf16[768,384]{1,0:T(8,128)(2,1)} %tangent_ref.1) | copy-start | bytes 1769476

commit v8 on v7

--- a/solution.py
+++ b/solution.py
@@ -82,7 +82,8 @@
     joined = jnp.concatenate([first_weight, first_tangent], axis=1)
     summed = scatter_sum_col(dot(gathered, joined, 1, 0))
     own_activation, derivative, own_tangent = activate(summed[:, :width], summed[:, width:])
-    acts = gather_col(jnp.concatenate([own_activation, own_tangent], axis=1))
+    own_acts = jnp.concatenate([own_activation, own_tangent], axis=1)
+    acts = gather(lax.all_gather(own_acts, "z_hi", tiled=True), "x", 4)
     partial_out = call(out_kernel, token_count, second_weight.shape[1])(acts, second_weight, second_tangent)
     out_share = exchange_sum(scatter_sum(partial_out, ("y", "core"), 8), "z_lo", 4).astype(bf16)
     tangent_out = gather(out_share, ("y", "core"), 8)

time: 209 us -> 208 us (level)
  the two profiles are of different devices: /device:TPU:2 before, /device:TPU:32 now
where the time goes in v8:
time: 208 us; the launch traced here: 207 us
  blocking collectives  201 us (97%)
  Pallas kernels  2.47 us (1%)
    all_to_all x12, blocking collectives, swap(): return lax.all_to_all(blocks, axes, 0, 0, tiled=True)  181 us
    all_gather x1, blocking collectives, shards(): acts = gather(lax.all_gather(own_acts, 'z_hi', tiled=True), 'x', 4)  19.3 us

profile of v8, /device:TPU:32, one launch (start us, length us, event | category | flops | bytes accessed | tf_op | source)
XLA Modules:
  0.0 206.7 jit_solution(10240033628356846022)
XLA Ops:
  0.6 0.0 copy-start.2
  0.6 0.0 copy-start.3
  0.6 0.8 broadcast_in_dim.18
  1.5 10.1 %all_to_all.95 = bf16[8,12,384]{2,1,0:T(8,128)(2,1)S(1)} all-to-all(bf16[8,12,384]{2,1,0:T(8,128)(2,1)S(1)} %broadcast_in_dim.18), channel_id=1, replica_groups=mesh['z_lo'=4,'y'=4,'core'=2,'x'=4,'z_hi'=4] {'y','core'}, dimensions={0} | all-to-all | bytes 147456 | tf_op jit(solution)/shard_map/all_to_all | solution.py:25
  11.6 14.1 %all_to_all.96 = bf16[4,96,384]{2,1,0:T(8,128)(2,1)S(1)} all-to-all(bf16[4,96,384]{2,1,0:T(8,128)(2,1)S(1)} %broadcast_in_dim.20), channel_id=1, replica_groups=mesh['z_lo'=4,'y'=4,'core'=2,'x'=4,'z_hi'=4] {'z_lo'}, dimensions={0} | all-to-all | bytes 589824 | tf_op jit(solution)/shard_map/all_to_all | solution.py:25
  25.7 0.0 copy-done.2
  25.7 0.0 copy-done.3
  25.7 0.8 convolution_convert_fusion
  26.5 18.2 %all_to_all.97 = bf16[4,96,1536]{2,1,0:T(8,128)(2,1)S(1)} all-to-all(bf16[4,96,1536]{2,1,0:T(8,128)(2,1)S(1)} %bitcast.24), channel_id=1, replica_groups=mesh['z_lo'=4,'y'=4,'core'=2,'x'=4,'z_hi'=4] {'x'}, dimensions={0} | all-to-all | bytes 2359296 | tf_op jit(solution)/shard_map/all_to_all | solution.py:25
  44.7 0.2 reduce_sum.66
  44.9 32.2 %all_to_all.98 = bf16[4,24,1536]{2,1,0:T(8,128)(2,1)S(1)} all-to-all(bf16[4,24,1536]{2,1,0:T(8,128)(2,1)S(1)} %bitcast.25), channel_id=1, replica_groups=mesh['z_lo'=4,'y'=4,'core'=2,'x'=4,'z_hi'=4] {'z_hi'}, dimensions={0} | all-to-all | bytes 589824 | tf_op jit(solution)/shard_map/all_to_all | solution.py:25
  77.1 0.1 multiply_convert_fusion.1
  77.2 19.3 %all_gather.3 = bf16[96,1536]{1,0:T(8,128)(2,1)S(1)} all-gather(bf16[24,1536]{1,0:T(8,128)(2,1)S(1)} %pad_maximum_fusion), channel_id=1, replica_groups=mesh['z_lo'=4,'y'=4,'core'=2,'x'=4,'z_hi'=4] {'z_hi'}, dimensions={0}, use_global_device_ids=true | all-gather | bytes 368640 | tf_op jit(solution)/shard_map/all_gather | solution.py:86
  96.5 0.1 broadcast_in_dim.21
  96.6 0.0 copy-start
  96.6 0.0 copy-start.1
  96.6 14.2 %all_to_all.99 = bf16[4,96,1536]{2,1,0:T(8,128)(2,1)S(1)} all-to-all(bf16[4,96,1536]{2,1,0:T(8,128)(2,1)S(1)} %broadcast_in_dim.21), channel_id=1, replica_groups=mesh['z_lo'=4,'y'=4,'core'=2,'x'=4,'z_hi'=4] {'x'}, dimensions={0} | all-to-all | bytes 2359296 | tf_op jit(solution)/shard_map/all_to_all | solution.py:25
  110.7 0.0 copy-done
  110.8 0.0 copy-done.1
  110.8 0.8 shard_map.68
  111.5 10.3 %all_to_all.100 = bf16[8,48,384]{2,1,0:T(8,128)(2,1)S(1)} all-to-all(bf16[8,48,384]{2,1,0:T(8,128)(2,1)S(1)} %bitcast.22), channel_id=1, replica_groups=mesh['z_lo'=4,'y'=4,'core'=2,'x'=4,'z_hi'=4] {'y','core'}, dimensions={0} | all-to-all | bytes 589824 | tf_op jit(solution)/shard_map/all_to_all | solution.py:25
  121.9 9.9 %all_to_all.101 = bf16[4,48,384]{2,1,0:T(8,128)(2,1)S(1)} all-to-all(bf16[4,48,384]{2,1,0:T(8,128)(2,1)S(1)} %broadcast_in_dim.22), channel_id=1, replica_groups=mesh['z_lo'=4,'y'=4,'core'=2,'x'=4,'z_hi'=4] {'z_lo'}, dimensions={0} | all-to-all | bytes 294912 | tf_op jit(solution)/shard_map/all_to_all | solution.py:25
  131.8 10.3 %all_to_all.102 = bf16[8,48,384]{2,1,0:T(8,128)(2,1)S(1)} all-to-all(bf16[8,48,384]{2,1,0:T(8,128)(2,1)S(1)} %broadcast_in_dim.23), channel_id=1, replica_groups=mesh['z_lo'=4,'y'=4,'core'=2,'x'=4,'z_hi'=4] {'y','core'}, dimensions={0} | all-to-all | bytes 589824 | tf_op jit(solution)/shard_map/all_to_all | solution.py:25
  142.1 0.5 convolution_convert_fusion.1
  142.6 13.0 %all_to_all.103 = bf16[4,96,768]{2,1,0:T(8,128)(2,1)S(1)} all-to-all(bf16[4,96,768]{2,1,0:T(8,128)(2,1)S(1)} %bitcast.23), channel_id=1, replica_groups=mesh['z_lo'=4,'y'=4,'core'=2,'x'=4,'z_hi'=4] {'x'}, dimensions={0} | all-to-all | bytes 1179648 | tf_op jit(solution)/shard_map/all_to_all | solution.py:25
  155.6 0.1 reduce_sum.70
  155.6 20.6 %all_to_all.104 = bf16[4,24,768]{2,1,0:T(8,128)(2,1)S(1)} all-to-all(bf16[4,24,768]{2,1,0:T(8,128)(2,1)S(1)} %bitcast.26), channel_id=1, replica_groups=mesh['z_lo'=4,'y'=4,'core'=2,'x'=4,'z_hi'=4] {'z_hi'}, dimensions={0} | all-to-all | bytes 294912 | tf_op jit(solution)/shard_map/all_to_all | solution.py:25
  176.2 0.1 multiply_convert_fusion
  176.3 17.7 %all_to_all.105 = bf16[4,24,768]{2,1,0:T(8,128)(2,1)S(1)} all-to-all(bf16[4,24,768]{2,1,0:T(8,128)(2,1)S(1)} %broadcast_in_dim.24), channel_id=1, replica_groups=mesh['z_lo'=4,'y'=4,'core'=2,'x'=4,'z_hi'=4] {'z_hi'}, dimensions={0} | all-to-all | bytes 294912 | tf_op jit(solution)/shard_map/all_to_all | solution.py:25
  194.1 10.9 %all_to_all.106 = bf16[4,96,768]{2,1,0:T(8,128)(2,1)S(1)} all-to-all(bf16[4,96,768]{2,1,0:T(8,128)(2,1)S(1)} %broadcast_in_dim.26), channel_id=1, replica_groups=mesh['z_lo'=4,'y'=4,'core'=2,'x'=4,'z_hi'=4] {'x'}, dimensions={0} | all-to-all | bytes 1179648 | tf_op jit(solution)/shard_map/all_to_all | solution.py:25
  205.0 1.7 shard_map.69
  (11 shorter events, 0.3 us)
Async XLA Ops:
  0.6 25.1 %copy-start.2 = (bf16[384,768]{1,0:T(8,128)(2,1)S(1)}, bf16[384,768]{1,0:T(8,128)(2,1)}, u32[]{:S(2)}) copy-start(bf16[384,768]{1,0:T(8,128)(2,1)} %param.7) | copy-start | bytes 1769476
  0.6 25.1 %copy-start.3 = (bf16[384,768]{1,0:T(8,128)(2,1)S(1)}, bf16[384,768]{1,0:T(8,128)(2,1)}, u32[]{:S(2)}) copy-start(bf16[384,768]{1,0:T(8,128)(2,1)} %param.6) | copy-start | bytes 1769476
  96.6 14.2 %copy-start = (bf16[768,384]{1,0:T(8,128)(2,1)S(1)}, bf16[768,384]{1,0:T(8,128)(2,1)}, u32[]{:S(2)}) copy-start(bf16[768,384]{1,0:T(8,128)(2,1)} %weight_ref.1) | copy-start | bytes 1769476
  96.6 14.2 %copy-start.1 = (bf16[768,384]{1,0:T(8,128)(2,1)S(1)}, bf16[768,384]{1,0:T(8,128)(2,1)}, u32[]{:S(2)}) copy-start(bf16[768,384]{1,0:T(8,128)(2,1)} %tangent_ref.1) | copy-start | bytes 1769476

commit v9 on v8

--- a/solution.py
+++ b/solution.py
@@ -58,10 +58,16 @@
     return (activation, derivative, tangent_act)
 
 
-def last_kernel(scaling, tokens_ref, grad_ref, acts_ref, outs_ref, first_ref, second_ref):
-    width = second_ref.shape[0]
-    second_ref[...] = (dot(acts_ref[:, :width], outs_ref[...], 0, 0) * scaling).astype(bf16)
-    first_ref[...] = (dot(tokens_ref[...], grad_ref[...], 0, 0) * scaling).astype(bf16)
+def last_kernel(scaling, tokens_ref, grad_ref, acts_ref, outs_ref, first_ref, second_ref, first, second, sems):
+    width = second.shape[0]
+    second[...] = (dot(acts_ref[:, :width], outs_ref[...], 0, 0) * scaling).astype(bf16)
+    second_out = pltpu.make_async_copy(second, second_ref, sems.at[0])
+    second_out.start()
+    first[...] = (dot(tokens_ref[...], grad_ref[...], 0, 0) * scaling).astype(bf16)
+    first_out = pltpu.make_async_copy(first, first_ref, sems.at[1])
+    first_out.start()
+    second_out.wait()
+    first_out.wait()
 
 
 def out_kernel(acts_ref, weight_ref, tangent_ref, out_ref):
@@ -93,11 +99,17 @@
     features = gathered.shape[1]
     first_shape = jax.ShapeDtypeStruct((features, width), bf16)
     second_shape = jax.ShapeDtypeStruct((width, features), bf16)
-    return pl.pallas_call(
+    return tuple(pl.pallas_call(
         functools.partial(last_kernel, scaling),
-        out_shape=(first_shape, second_shape),
+        out_shape=[first_shape, second_shape],
+        out_specs=[pl.BlockSpec(memory_space=pl.ANY)] * 2,
+        scratch_shapes=[
+            pltpu.VMEM((features, width), bf16),
+            pltpu.VMEM((width, features), bf16),
+            pltpu.SemaphoreType.DMA((2,)),
+        ],
         compiler_params=pltpu.CompilerParams(vmem_limit_bytes=16 * 1024 * 1024),
-    )(gathered, grad_pre, acts, tangent_out)
+    )(gathered, grad_pre, acts, tangent_out))
 
 
 def solution(mesh):

time: 208 us -> 208 us (level)
  the two profiles are of different devices: /device:TPU:32 before, /device:TPU:40 now
where the time goes in v9:
time: 208 us; the launch traced here: 207 us
  blocking collectives  201 us (97%)
  Pallas kernels  2.49 us (1%)
    all_to_all x12, blocking collectives, swap(): return lax.all_to_all(blocks, axes, 0, 0, tiled=True)  182 us
    all_gather x1, blocking collectives, shards(): acts = gather(lax.all_gather(own_acts, 'z_hi', tiled=True), 'x', 4)  18.8 us

profile of v9, /device:TPU:40, one launch (start us, length us, event | category | flops | bytes accessed | tf_op | source)
XLA Modules:
  0.0 207.0 jit_solution(9909814906214078096)
XLA Ops:
  0.6 0.0 copy-start.2
  0.6 0.0 copy-start.3
  0.6 0.8 broadcast_in_dim.18
  1.5 9.1 %all_to_all.95 = bf16[8,12,384]{2,1,0:T(8,128)(2,1)S(1)} all-to-all(bf16[8,12,384]{2,1,0:T(8,128)(2,1)S(1)} %broadcast_in_dim.18), channel_id=1, replica_groups=mesh['z_lo'=4,'y'=4,'core'=2,'x'=4,'z_hi'=4] {'y','core'}, dimensions={0} | all-to-all | bytes 147456 | tf_op jit(solution)/shard_map/all_to_all | solution.py:25
  10.6 14.1 %all_to_all.96 = bf16[4,96,384]{2,1,0:T(8,128)(2,1)S(1)} all-to-all(bf16[4,96,384]{2,1,0:T(8,128)(2,1)S(1)} %broadcast_in_dim.20), channel_id=1, replica_groups=mesh['z_lo'=4,'y'=4,'core'=2,'x'=4,'z_hi'=4] {'z_lo'}, dimensions={0} | all-to-all | bytes 589824 | tf_op jit(solution)/shard_map/all_to_all | solution.py:25
  24.7 0.0 copy-done.2
  24.7 0.0 copy-done.3
  24.7 0.8 convolution_convert_fusion
  25.5 18.2 %all_to_all.97 = bf16[4,96,1536]{2,1,0:T(8,128)(2,1)S(1)} all-to-all(bf16[4,96,1536]{2,1,0:T(8,128)(2,1)S(1)} %bitcast.24), channel_id=1, replica_groups=mesh['z_lo'=4,'y'=4,'core'=2,'x'=4,'z_hi'=4] {'x'}, dimensions={0} | all-to-all | bytes 2359296 | tf_op jit(solution)/shard_map/all_to_all | solution.py:25
  43.7 0.2 reduce_sum.66
  43.9 32.2 %all_to_all.98 = bf16[4,24,1536]{2,1,0:T(8,128)(2,1)S(1)} all-to-all(bf16[4,24,1536]{2,1,0:T(8,128)(2,1)S(1)} %bitcast.25), channel_id=1, replica_groups=mesh['z_lo'=4,'y'=4,'core'=2,'x'=4,'z_hi'=4] {'z_hi'}, dimensions={0} | all-to-all | bytes 589824 | tf_op jit(solution)/shard_map/all_to_all | solution.py:25
  76.1 0.1 multiply_convert_fusion.1
  76.2 18.8 %all_gather.3 = bf16[96,1536]{1,0:T(8,128)(2,1)S(1)} all-gather(bf16[24,1536]{1,0:T(8,128)(2,1)S(1)} %pad_maximum_fusion), channel_id=1, replica_groups=mesh['z_lo'=4,'y'=4,'core'=2,'x'=4,'z_hi'=4] {'z_hi'}, dimensions={0}, use_global_device_ids=true | all-gather | bytes 368640 | tf_op jit(solution)/shard_map/all_gather | solution.py:92
  95.0 0.1 broadcast_in_dim.21
  95.1 0.0 copy-start
  95.1 0.0 copy-start.1
  95.1 14.2 %all_to_all.99 = bf16[4,96,1536]{2,1,0:T(8,128)(2,1)S(1)} all-to-all(bf16[4,96,1536]{2,1,0:T(8,128)(2,1)S(1)} %broadcast_in_dim.21), channel_id=1, replica_groups=mesh['z_lo'=4,'y'=4,'core'=2,'x'=4,'z_hi'=4] {'x'}, dimensions={0} | all-to-all | bytes 2359296 | tf_op jit(solution)/shard_map/all_to_all | solution.py:25
  109.3 0.0 copy-done
  109.3 0.0 copy-done.1
  109.3 0.8 shard_map.68
  110.1 10.7 %all_to_all.100 = bf16[8,48,384]{2,1,0:T(8,128)(2,1)S(1)} all-to-all(bf16[8,48,384]{2,1,0:T(8,128)(2,1)S(1)} %bitcast.22), channel_id=1, replica_groups=mesh['z_lo'=4,'y'=4,'core'=2,'x'=4,'z_hi'=4] {'y','core'}, dimensions={0} | all-to-all | bytes 589824 | tf_op jit(solution)/shard_map/all_to_all | solution.py:25
  120.9 9.9 %all_to_all.101 = bf16[4,48,384]{2,1,0:T(8,128)(2,1)S(1)} all-to-all(bf16[4,48,384]{2,1,0:T(8,128)(2,1)S(1)} %broadcast_in_dim.22), channel_id=1, replica_groups=mesh['z_lo'=4,'y'=4,'core'=2,'x'=4,'z_hi'=4] {'z_lo'}, dimensions={0} | all-to-all | bytes 294912 | tf_op jit(solution)/shard_map/all_to_all | solution.py:25
  130.8 10.3 %all_to_all.102 = bf16[8,48,384]{2,1,0:T(8,128)(2,1)S(1)} all-to-all(bf16[8,48,384]{2,1,0:T(8,128)(2,1)S(1)} %broadcast_in_dim.23), channel_id=1, replica_groups=mesh['z_lo'=4,'y'=4,'core'=2,'x'=4,'z_hi'=4] {'y','core'}, dimensions={0} | all-to-all | bytes 589824 | tf_op jit(solution)/shard_map/all_to_all | solution.py:25
  141.1 0.5 convolution_convert_fusion.1
  141.6 12.9 %all_to_all.103 = bf16[4,96,768]{2,1,0:T(8,128)(2,1)S(1)} all-to-all(bf16[4,96,768]{2,1,0:T(8,128)(2,1)S(1)} %bitcast.23), channel_id=1, replica_groups=mesh['z_lo'=4,'y'=4,'core'=2,'x'=4,'z_hi'=4] {'x'}, dimensions={0} | all-to-all | bytes 1179648 | tf_op jit(solution)/shard_map/all_to_all | solution.py:25
  154.5 0.1 reduce_sum.70
  154.6 20.6 %all_to_all.104 = bf16[4,24,768]{2,1,0:T(8,128)(2,1)S(1)} all-to-all(bf16[4,24,768]{2,1,0:T(8,128)(2,1)S(1)} %bitcast.26), channel_id=1, replica_groups=mesh['z_lo'=4,'y'=4,'core'=2,'x'=4,'z_hi'=4] {'z_hi'}, dimensions={0} | all-to-all | bytes 294912 | tf_op jit(solution)/shard_map/all_to_all | solution.py:25
  175.2 0.1 multiply_convert_fusion
  175.3 17.6 %all_to_all.105 = bf16[4,24,768]{2,1,0:T(8,128)(2,1)S(1)} all-to-all(bf16[4,24,768]{2,1,0:T(8,128)(2,1)S(1)} %broadcast_in_dim.24), channel_id=1, replica_groups=mesh['z_lo'=4,'y'=4,'core'=2,'x'=4,'z_hi'=4] {'z_hi'}, dimensions={0} | all-to-all | bytes 294912 | tf_op jit(solution)/shard_map/all_to_all | solution.py:25
  193.0 12.3 %all_to_all.106 = bf16[4,96,768]{2,1,0:T(8,128)(2,1)S(1)} all-to-all(bf16[4,96,768]{2,1,0:T(8,128)(2,1)S(1)} %broadcast_in_dim.26), channel_id=1, replica_groups=mesh['z_lo'=4,'y'=4,'core'=2,'x'=4,'z_hi'=4] {'x'}, dimensions={0} | all-to-all | bytes 1179648 | tf_op jit(solution)/shard_map/all_to_all | solution.py:25
  205.3 1.7 shard_map.69
  (11 shorter events, 0.3 us)
Async XLA Ops:
  0.6 24.1 %copy-start.2 = (bf16[384,768]{1,0:T(8,128)(2,1)S(1)}, bf16[384,768]{1,0:T(8,128)(2,1)}, u32[]{:S(2)}) copy-start(bf16[384,768]{1,0:T(8,128)(2,1)} %param.7) | copy-start | bytes 1769476
  0.6 24.1 %copy-start.3 = (bf16[384,768]{1,0:T(8,128)(2,1)S(1)}, bf16[384,768]{1,0:T(8,128)(2,1)}, u32[]{:S(2)}) copy-start(bf16[384,768]{1,0:T(8,128)(2,1)} %param.6) | copy-start | bytes 1769476
  95.1 14.2 %copy-start = (bf16[768,384]{1,0:T(8,128)(2,1)S(1)}, bf16[768,384]{1,0:T(8,128)(2,1)}, u32[]{:S(2)}) copy-start(bf16[768,384]{1,0:T(8,128)(2,1)} %weight_ref.1) | copy-start | bytes 1769476
  95.1 14.2 %copy-start.1 = (bf16[768,384]{1,0:T(8,128)(2,1)S(1)}, bf16[768,384]{1,0:T(8,128)(2,1)}, u32[]{:S(2)}) copy-start(bf16[768,384]{1,0:T(8,128)(2,1)} %tangent_ref.1) | copy-start | bytes 1769476
